TPU v7x, 256 devices: a whole 4x4x8 slice. The times are simulated.
256 devices in a mesh: role: 2 (over y_lo), proto: 64 (over x, y_hi, z), crop: 2 (over core).
Axes of the slice: x: 4, y: 4 (y_hi: 2, y_lo: 2; y = y_hi * 2 + y_lo), z: 8, core: 2. Of those that a mesh axis runs over, the one named last changes fastest.
Arguments:
- embeddings: bfloat16 [2, 1024, 512], P('role', 'crop'), may hold values from -1 to 1, as said below
- weights: bfloat16 [2, 512, 262144], P('role', None, 'proto'), may hold values from -1 to 1, as said below
Outputs:
- weight_grad: bfloat16 [2, 2, 128, 262144], P('crop', 'role', None, 'proto')
- embed_grad: bfloat16 [2, 512, 512], P('crop', 'proto', 'role')
Inputs may be any that keep to these rules, and one draw needn't show every extreme that they name: `embeddings`: each crop's row has unit Euclidean length before rounding to bfloat16. `weights`: each prototype column has unit Euclidean length before rounding to bfloat16.
All inputs are finite; a program needn't handle non-finite values.
Results may differ from a plain program's by a relative error of at most 0.001.
The roundings to bfloat16 on the way count: a program that leaves them out, or rounds other values in their place, can miss the bound.
Values may be sent and summed in bfloat16 or wider, within the bound.
A program may use at most 128 MiB of HBM per device.

v0:
```python
import jax
import jax.numpy as jnp
from jax import lax
from jax.sharding import PartitionSpec as P

ITERS = 3


def sent_to_all(x, axis):
    copies = jnp.broadcast_to(x, (lax.axis_size(axis), *x.shape))
    return lax.all_to_all(copies, axis, split_axis=0, concat_axis=0, tiled=True)


def of_everyone(x, axis):
    return sent_to_all(x, axis).sum(axis=0)


def passed_along(value, axis, steps):
    count = lax.axis_size(axis)
    first, last = (max(0, -steps), min(count, count - steps))
    return lax.ppermute(value, axis, [(source, source + steps) for source in range(first, last)])


def in_blocks(x, dim, peers):
    before, after = (x.shape[:dim], x.shape[dim + 1 :])
    return jnp.moveaxis(x.reshape(*before, peers, -1, *after), dim, 0)


def sum_at_owner(x, axis, dim):
    peers = lax.axis_size(axis)
    blocks = lax.all_to_all(in_blocks(x, dim, peers), axis, 0, 0, tiled=True)
    return jnp.sum(blocks, axis=0)


def per_device(embeddings, weights):
    role_place = lax.axis_index("role")
    learner_indicator = role_place == 1
    own_embed = embeddings[0]
    own_weight = weights[0]
    row_number = own_embed.shape[0]
    feature_width = own_embed.shape[1]
    quarter_slice = feature_width // 4
    half_width = feature_width // 2
    block_width = own_weight.shape[1]
    similarity_array = jnp.dot(own_embed, own_weight, preferred_element_type=jnp.float32)
    sharpening_divisor = jnp.where(learner_indicator, 0.1, 0.07).astype(jnp.float32)
    unnormalized_array = similarity_array / sharpening_divisor
    row_shift = jnp.zeros((row_number,), jnp.float32)
    column_shift = jnp.zeros((block_width,), jnp.float32)
    for iteration in range(ITERS):
        column_totals_list = of_everyone(
            jnp.sum(jnp.exp(unnormalized_array + row_shift[:, None]), axis=0), "crop"
        )
        column_shift = jnp.where(learner_indicator, 0.0, -jnp.log(column_totals_list))
        row_sums = of_everyone(
            jnp.sum(jnp.exp(unnormalized_array + column_shift[None, :]), axis=1), "proto"
        )
        row_shift = -jnp.log(row_sums)
    tempered = jnp.exp(unnormalized_array + column_shift[None, :] + row_shift[:, None])
    targets = tempered.astype(jnp.bfloat16)
    received_parts = passed_along(targets, "role", 1)
    logit_grads = ((tempered - received_parts.astype(jnp.float32)) / 0.1).astype(jnp.bfloat16)

    def no_weight_terms():
        return jnp.zeros((feature_width, block_width), jnp.float32)

    def student_terms():
        return lax.dot_general(
            own_embed, logit_grads, (((0,), (0,)), ((), ())), preferred_element_type=jnp.float32
        )

    partial_value = lax.cond(learner_indicator, student_terms, no_weight_terms)
    halves = sum_at_owner(partial_value, "crop", 0).astype(jnp.bfloat16)
    quarters = halves.reshape(2, quarter_slice, block_width)
    arrived = passed_along(quarters[0], "role", -1)
    weight_block = jnp.where(learner_indicator, quarters[1], arrived)
    weight_block = weight_block.reshape(1, 1, quarter_slice, block_width)
    owned_rows = row_number // lax.axis_size("proto")

    def compute():
        return lax.dot_general(
            logit_grads, own_weight, (((1,), (1,)), ((), ())), preferred_element_type=jnp.float32
        )

    def empty_terms():
        return jnp.zeros((owned_rows * lax.axis_size("proto"), feature_width), jnp.float32)

    summed = sum_at_owner(lax.cond(learner_indicator, compute, empty_terms), "proto", 0).astype(
        jnp.bfloat16
    )
    teacher_columns = passed_along(summed[:, :half_width], "role", -1)
    representation_tile = jnp.where(learner_indicator, summed[:, half_width:], teacher_columns)[
        None
    ]
    return (weight_block, representation_tile)


def solution(mesh):
    placed = (P("role", "crop", None), P("role", None, "proto"))
    return jax.shard_map(
        per_device,
        mesh=mesh,
        in_specs=placed,
        out_specs=(P("crop", "role", None, "proto"), P("crop", "proto", "role")),
        check_vma=False,
    )
```

profile of v0, /device:TPU:1, one launch (start us, length us, event | category | flops | bytes accessed | tf_op | source)
XLA Modules:
  0.0 283.1 jit_solution(13911016526594536740)
XLA Ops:
  0.6 8.0 %exponential_reduce_fusion.5 = (f32[4096]{0:T(1024)S(1)}, f32[512,4096]{1,0:T(8,128)}) fusion(f32[]{:T(128)S(6)} %select_n.49, bf16[1,512,4096]{2,1,0:T(8,128)(2,1)} %param.7, bf16[1,512,512]{2,1,0:T(8,128)(2,1)} %param.6), kind=kOutput, calls=%fused_computation.7 | convolution fusion | flops 2151673856 | bytes 13123588 | tf_op jit(solution)/shard_map/dot_general | solution.py:45
  8.6 6.6 %all_to_all.46 = f32[2,1,4096]{2,1,0:T(1,128)S(1)} all-to-all(f32[2,1,4096]{2,1,0:T(1,128)S(1)} %broadcast_in_dim.35), channel_id=1, replica_groups=mesh['role'=2,'proto'=64,'crop'=2] {'crop'}, dimensions={0} | all-to-all | bytes 65536 | tf_op jit(solution)/shard_map/all_to_all | solution.py:11
  15.3 4.6 %exponential_reduce_fusion.4 = f32[512]{0:T(512)S(1)} fusion(f32[512,4096]{1,0:T(8,128)} %get-tuple-element.21, f32[4096]{0:T(1024)S(1)} %negate_select_fusion.2), kind=kLoop, calls=%fused_computation.6 | loop fusion | flops 4193792 | bytes 8407040 | tf_op jit(solution)/shard_map/reduce_sum | solution.py:56
  20.1 23.8 %all_to_all.47 = f32[64,1,512]{2,1,0:T(1,128)S(1)} all-to-all(f32[64,1,512]{2,1,0:T(1,128)S(1)} %broadcast_in_dim.36), channel_id=1, replica_groups=mesh['role'=2,'proto'=64,'crop'=2] {'proto'}, dimensions={0} | all-to-all | bytes 262144 | tf_op jit(solution)/shard_map/all_to_all | solution.py:11
  44.0 4.7 %exponential_reduce_fusion.3 = f32[4096]{0:T(1024)S(1)} fusion(f32[512,4096]{1,0:T(8,128)} %get-tuple-element.21, f32[512]{0:T(512)S(1)} %log_negate_fusion.2), kind=kLoop, calls=%fused_computation.5 | loop fusion | flops 4190208 | bytes 8407040 | tf_op jit(solution)/shard_map/reduce_sum | solution.py:52
  48.8 5.5 %all_to_all.48 = f32[2,1,4096]{2,1,0:T(1,128)S(1)} all-to-all(f32[2,1,4096]{2,1,0:T(1,128)S(1)} %broadcast_in_dim.37), channel_id=1, replica_groups=mesh['role'=2,'proto'=64,'crop'=2] {'crop'}, dimensions={0} | all-to-all | bytes 65536 | tf_op jit(solution)/shard_map/all_to_all | solution.py:11
  54.3 4.6 %exponential_reduce_fusion.2 = f32[512]{0:T(512)S(1)} fusion(f32[512,4096]{1,0:T(8,128)} %get-tuple-element.21, f32[4096]{0:T(1024)S(1)} %negate_select_fusion.1), kind=kLoop, calls=%fused_computation.4 | loop fusion | flops 4193792 | bytes 8407040 | tf_op jit(solution)/shard_map/reduce_sum | solution.py:56
  59.0 15.6 %all_to_all.49 = f32[64,1,512]{2,1,0:T(1,128)S(1)} all-to-all(f32[64,1,512]{2,1,0:T(1,128)S(1)} %broadcast_in_dim.38), channel_id=1, replica_groups=mesh['role'=2,'proto'=64,'crop'=2] {'proto'}, dimensions={0} | all-to-all | bytes 262144 | tf_op jit(solution)/shard_map/all_to_all | solution.py:11
  74.8 4.7 %exponential_reduce_fusion.1 = f32[4096]{0:T(1024)S(1)} fusion(f32[512,4096]{1,0:T(8,128)} %get-tuple-element.21, f32[512]{0:T(512)S(1)} %log_negate_fusion.1), kind=kLoop, calls=%fused_computation.3 | loop fusion | flops 4190208 | bytes 8407040 | tf_op jit(solution)/shard_map/reduce_sum | solution.py:52
  79.5 5.1 %all_to_all.50 = f32[2,1,4096]{2,1,0:T(1,128)S(1)} all-to-all(f32[2,1,4096]{2,1,0:T(1,128)S(1)} %broadcast_in_dim.39), channel_id=1, replica_groups=mesh['role'=2,'proto'=64,'crop'=2] {'crop'}, dimensions={0} | all-to-all | bytes 65536 | tf_op jit(solution)/shard_map/all_to_all | solution.py:11
  84.7 4.6 %exponential_reduce_fusion = f32[512]{0:T(512)S(1)} fusion(f32[512,4096]{1,0:T(8,128)} %get-tuple-element.21, f32[4096]{0:T(1024)S(1)} %negate_select_fusion), kind=kLoop, calls=%fused_computation.2 | loop fusion | flops 4193792 | bytes 8407040 | tf_op jit(solution)/shard_map/reduce_sum | solution.py:56
  89.4 15.9 %all_to_all.51 = f32[64,1,512]{2,1,0:T(1,128)S(1)} all-to-all(f32[64,1,512]{2,1,0:T(1,128)S(1)} %broadcast_in_dim.40), channel_id=1, replica_groups=mesh['role'=2,'proto'=64,'crop'=2] {'proto'}, dimensions={0} | all-to-all | bytes 262144 | tf_op jit(solution)/shard_map/all_to_all | solution.py:11
  105.4 6.8 %fusion = bf16[512,4096]{1,0:T(8,128)(2,1)} fusion(f32[512,4096]{1,0:T(8,128)} %get-tuple-element.21, f32[512]{0:T(512)S(1)} %log_negate_fusion, f32[4096]{0:T(1024)S(1)} %negate_select_fusion), kind=kLoop, calls=%fused_computation.8 | loop fusion | flops 6291456 | bytes 12601344 | tf_op jit(solution)/shard_map/convert_element_type | solution.py:60
  112.2 4.3 %collective-permute-start = (bf16[512,4096]{1,0:T(8,128)(2,1)}, bf16[512,4096]{1,0:T(8,128)(2,1)}, u32[]{:S(2)}, u32[]{:S(2)}) collective-permute-start(bf16[512,4096]{1,0:T(8,128)(2,1)} %fusion), channel_id=1, source_target_pairs={{0,128},{1,129},{2,130},{3,131},{4,132},{5,133},{6,134},{7,135},{8... | collective-permute-start | bytes 12582920 | tf_op jit(solution)/shard_map/ppermute | solution.py:21
  116.5 86.5 %collective-permute-done = bf16[512,4096]{1,0:T(8,128)(2,1)} collective-permute-done((bf16[512,4096]{1,0:T(8,128)(2,1)}, bf16[512,4096]{1,0:T(8,128)(2,1)}, u32[]{:S(2)}, u32[]{:S(2)}) %collective-permute-start) | collective-permute-done | bytes 4194336 | tf_op jit(solution)/shard_map/ppermute | solution.py:21
  203.0 7.1 %multiply_convert_fusion = bf16[512,4096]{1,0:T(8,128)(2,1)} fusion(bf16[512,4096]{1,0:T(8,128)(2,1)} %collective-permute-done, f32[512,4096]{1,0:T(8,128)} %get-tuple-element.21, f32[512]{0:T(512)S(1)} %log_negate_fusion, f32[4096]{0:T(1024)S(1)} %negate_select_fusion), kind=kLoop, calls=%fused_computation | loop fusion | flops 12582912 | bytes 16795648 | tf_op jit(solution)/shard_map/convert_element_type | solution.py:62
  210.1 4.2 %conditional.2 = (f32[512,4096]{1,0:T(8,128)}) conditional(s32[]{:T(128)} %convert_element_type.19, () %tuple.20, (bf16[512,512]{1,0:T(8,128)(2,1)S(1)}, bf16[512,4096]{1,0:T(8,128)(2,1)}) %tuple.30), branch_computations={%region_12.13_spmd, %region_13.14_spmd} | conditional | flops 2147483648 | bytes 13107208 | solution.py:72
  210.1 4.2 %broadcast.47 = f32[512,4096]{1,0:T(8,128)} broadcast(f32[]{:T(128)} %constant.3.clone), dimensions={} | broadcast | bytes 8388612 | tf_op jit(solution)/shard_map/broadcast.1
  214.3 9.5 %all-to-all-start.6 = ((f32[2,256,4096]{2,1,0:T(8,128)}), f32[2,256,4096]{2,1,0:T(8,128)}, u32[]{:S(2)}, u32[]{:S(2)}) async-start(f32[2,256,4096]{2,1,0:T(8,128)} %bitcast.20), calls=%async_computation.6 | async-start | bytes 16777216 | tf_op jit(solution)/shard_map/all_to_all | solution.py:31
  224.9 6.0 %all-to-all-done.6 = f32[2,256,4096]{2,1,0:T(8,128)} async-done(((f32[2,256,4096]{2,1,0:T(8,128)}), f32[2,256,4096]{2,1,0:T(8,128)}, u32[]{:S(2)}, u32[]{:S(2)}) %all-to-all-start.6) | async-done | bytes 8388640 | tf_op jit(solution)/shard_map/all_to_all | solution.py:31
  230.9 5.0 %all-to-all-start.7 = ((f32[64,8,512]{2,1,0:T(8,128)}), f32[64,8,512]{2,1,0:T(8,128)S(1)}, u32[]{:S(2)}, u32[]{:S(2)}) async-start(f32[64,8,512]{2,1,0:T(8,128)} %bitcast.4), calls=%async_computation.7 | async-start | bytes 2097152 | tf_op jit(solution)/shard_map/all_to_all | solution.py:31
  235.9 4.6 %reduce_sum.138 = bf16[256,4096]{1,0:T(8,128)(2,1)S(1)} reduce(f32[2,256,4096]{2,1,0:T(8,128)} %all-to-all-done.6, f32[]{:T(128)} %constant.19.clone.1), dimensions={0}, to_apply=%region_14.15 | reduce | flops 1048576 | bytes 10485764 | tf_op jit(solution)/shard_map/reduce_sum | solution.py:32
  242.9 20.6 %all-to-all-done.7 = f32[64,8,512]{2,1,0:T(8,128)S(1)} async-done(((f32[64,8,512]{2,1,0:T(8,128)}), f32[64,8,512]{2,1,0:T(8,128)S(1)}, u32[]{:S(2)}, u32[]{:S(2)}) %all-to-all-start.7) | async-done | bytes 1048608 | tf_op jit(solution)/shard_map/all_to_all | solution.py:31
  264.8 15.3 %collective-permute-done.1 = bf16[128,4096]{1,0:T(8,128)(2,1)} collective-permute-done((bf16[128,4096]{1,0:T(8,128)(2,1)}, bf16[128,4096]{1,0:T(8,128)(2,1)}, u32[]{:S(2)}, u32[]{:S(2)}) %collective-permute-start.1) | collective-permute-done | bytes 1048608 | tf_op jit(solution)/shard_map/ppermute | solution.py:21
  (30 shorter events, 9.6 us)
Async XLA Ops:
  112.2 90.8 %collective-permute-start = (bf16[512,4096]{1,0:T(8,128)(2,1)}, bf16[512,4096]{1,0:T(8,128)(2,1)}, u32[]{:S(2)}, u32[]{:S(2)}) collective-permute-start(bf16[512,4096]{1,0:T(8,128)(2,1)} %fusion), channel_id=1, source_target_pairs={{0,128},{1,129},{2,130},{3,131},{4,132},{5,133},{6,134},{7,135},{8... | collective-permute-start | bytes 12582920 | tf_op jit(solution)/shard_map/ppermute | solution.py:21
  116.5 93.6 %copy-start = (bf16[1,512,512]{2,1,0:T(8,128)(2,1)S(1)}, bf16[1,512,512]{2,1,0:T(8,128)(2,1)}, u32[]{:S(2)}) copy-start(bf16[1,512,512]{2,1,0:T(8,128)(2,1)} %param.6) | copy-start | bytes 1572868
  214.3 16.6 %all-to-all-start.6 = ((f32[2,256,4096]{2,1,0:T(8,128)}), f32[2,256,4096]{2,1,0:T(8,128)}, u32[]{:S(2)}, u32[]{:S(2)}) async-start(f32[2,256,4096]{2,1,0:T(8,128)} %bitcast.20), calls=%async_computation.6 | async-start | bytes 16777216 | tf_op jit(solution)/shard_map/all_to_all | solution.py:31
  230.9 32.5 %all-to-all-start.7 = ((f32[64,8,512]{2,1,0:T(8,128)}), f32[64,8,512]{2,1,0:T(8,128)S(1)}, u32[]{:S(2)}, u32[]{:S(2)}) async-start(f32[64,8,512]{2,1,0:T(8,128)} %bitcast.4), calls=%async_computation.7 | async-start | bytes 2097152 | tf_op jit(solution)/shard_map/all_to_all | solution.py:31
  241.6 38.6 %collective-permute-start.1 = (bf16[128,4096]{1,0:T(8,128)(2,1)}, bf16[128,4096]{1,0:T(8,128)(2,1)}, u32[]{:S(2)}, u32[]{:S(2)}) collective-permute-start(bf16[128,4096]{1,0:T(8,128)(2,1)} %slice.19), channel_id=1, source_target_pairs={{128,0},{129,1},{130,2},{131,3},{132,4},{133,5},{134,6},{135,7},{1... | collective-permute-start | bytes 3145736 | tf_op jit(solution)/shard_map/ppermute | solution.py:21
  263.5 18.9 %collective-permute-start.2 = (bf16[8,256]{1,0:T(8,128)(2,1)S(1)}, bf16[8,256]{1,0:T(8,128)(2,1)S(1)}, u32[]{:S(2)}, u32[]{:S(2)}) collective-permute-start(bf16[8,256]{1,0:T(8,128)(2,1)S(1)} %slice.21), channel_id=1, source_target_pairs={{128,0},{129,1},{130,2},{131,3},{132,4},{133,5},{134,6},{135,7},{1... | collective-permute-start | bytes 12296 | tf_op jit(solution)/shard_map/ppermute | solution.py:21
where the time goes:
time: 284 us; the launch traced here: 283 us
  waiting for transfers between devices  128 us (45%)
  blocking collectives  72.6 us (26%)
  other arithmetic  45.3 us (16%)
  starting transfers between devices  21.3 us (8%)
  matrix products  7.98 us (3%)
  local copies, waits for them, and re-layouts  6.66 us (2%)
    ppermute x3, waiting for transfers between devices, passed_along(): lax.ppermute(value, axis, [(source, source + steps) for source in range(f...  102 us
    all_to_all x6, blocking collectives, sent_to_all(): return lax.all_to_all(copies, axis, split_axis=0, concat_axis=0, tiled=True)  72.6 us
    all_to_all x2, waiting for transfers between devices, sum_at_owner(): blocks = lax.all_to_all(in_blocks(x, dim, peers), axis, 0, 0, tiled=True)  26.6 us
    all_to_all x2, starting transfers between devices, sum_at_owner(): blocks = lax.all_to_all(in_blocks(x, dim, peers), axis, 0, 0, tiled=True)  14.5 us
    reduce_sum x3, other arithmetic, per_device(): jnp.sum(jnp.exp(unnormalized_array + column_shift[None, :]), axis=1)  13.8 us
    reduce_sum x2, other arithmetic, per_device(): jnp.sum(jnp.exp(unnormalized_array + row_shift[:, None]), axis=0)  9.45 us
    dot_general x1, matrix products, per_device(): jnp.dot(own_embed, own_weight, preferred_element_type=jnp.float32)  7.98 us
    convert_element_type x1, other arithmetic, per_device(): ((tempered - received_parts.astype(jnp.float32)) / 0.1).astype(jnp.bfloat16)  7.06 us
  transfers between devices with their start and end apart: 5, of which 4 were waited for; matrix products, arithmetic and copies ran while one was open for 3% of the time, Pallas kernels for 0%

commit v1 on v0

v1 whole, which is shorter than its diff:
```python
import functools

import jax
import jax.numpy as jnp
from jax import lax
from jax.experimental import pallas as pl
from jax.experimental.pallas import tpu as pltpu
from jax.sharding import PartitionSpec as P

F32 = jnp.float32
BF16 = jnp.bfloat16
MESH = pl.DeviceIdType.MESH
LANES = 128
TILE = 256
CHIPS = {64: (4, 2, 8), 8: (2, 2, 2), 4: (2, 2, 1)}
R1, R2, R3, SINV = range(4)


def across(column, width):
    return jnp.concatenate([column] * (width // LANES), axis=1)


def kernel(chips, emb, wgt, wg_out, eg_out,
           EB, WB, AB, G, ET, U, RS, COL, SRC1, SRC2, AR1, AR2, MSRC, MSG,
           EGP, RC, RX, S1, RZ, S2, RY, WGB,
           loc, e_send, e_recv, w_send, w_recv, a1s, a1r, a2s, a2r, m_send, m_recv,
           c_send, c_recv, x_send, x_recv, z_send, z_recv, y_send, y_recv, g_send, g_recv, g_loc):
    nx, nyh, nz = chips
    role, p, c = (lax.axis_index(a) for a in ("role", "proto", "crop"))
    x, yh, z = p // (nyh * nz), (p // nz) % nyh, p % nz
    teacher = role == 0
    half, D = emb.shape[1], emb.shape[2]
    B = 2 * half
    PC = wgt.shape[2] // 2
    PG = PC // 2
    vrows = B // LANES
    owned = half // p_count(chips)
    quarter = D // 4

    def at(role_, x_, yh_, z_, c_):
        return {"role": role_, "proto": (x_ * nyh + yh_) * nz + z_, "crop": c_}

    def send(src, dst, s, r, to):
        copy = pltpu.make_async_remote_copy(
            src_ref=src, dst_ref=dst, send_sem=s, recv_sem=r, device_id=to, device_id_type=MESH)
        copy.start()
        return copy

    def arrived(ref, sem):
        pltpu.make_async_copy(ref, ref, sem).wait()

    other_core = at(role, x, yh, z, 1 - c)
    partner = at(1 - role, x, yh, z, c)
    wrap = at(1 - role, x, 1 - yh, z, c)

    n1, n2 = 2 * nz, nx * nyh
    id1, id2 = 2 * z + c, x * nyh + yh

    def peer1(d):
        j = (id1 + d) % n1
        return at(role, x, yh, j // 2, j % 2)

    def peer2(d):
        j = (id2 + d) % n2
        return at(role, j // nyh, j % nyh, z, c)

    barrier = pltpu.get_barrier_semaphore()

    def greet(to):
        pl.semaphore_signal(barrier, inc=1, device_id=to, device_id_type=MESH)

    for d in range(1, n1):
        greet(peer1(d))
    for d in range(1, n2):
        greet(peer2(d))
    greet(partner)
    greet(at(1 - role, x, yh, z, 1 - c))
    greet(wrap)
    own_e = pltpu.make_async_copy(emb.at[0], EB.at[role, pl.ds(pl.multiple_of(c * half, half), half)], loc.at[0])
    own_e.start()
    own_w = pltpu.make_async_copy(
        wgt.at[0, :, pl.ds(pl.multiple_of(c * PC, PC), PC)], WB.at[role], loc.at[1])
    own_w.start()
    pl.semaphore_wait(barrier, n1 - 1 + n2 - 1 + 3)

    my_half = pl.ds(pl.multiple_of(c * half, half), half)
    e_core = send(emb.at[0], EB.at[role, my_half], e_send.at[0], e_recv.at[0], other_core)
    e_wrap = send(emb.at[0], EB.at[role, my_half], e_send.at[1], e_recv.at[1], wrap)
    away = pl.multiple_of((1 - role) * PG, PG)
    w_swap = send(
        wgt.at[0, :, pl.ds(pl.multiple_of(c * PC + (1 - role) * PG, PG), PG)],
        WB.at[role, :, pl.ds(away, PG)], w_send.at[0], w_recv.at[0], partner)

    gcols = pl.ds(pl.multiple_of(role * PG, PG), PG)
    inv_t, inv_s = 1.0 / 0.07, 1.0 / 0.1
    scale = jnp.where(teacher, inv_t, inv_s).astype(F32)
    other_scale = jnp.where(teacher, inv_s, inv_t).astype(F32)

    def expand(ref, slot):
        for i in range(vrows):
            COL[slot, i * LANES:(i + 1) * LANES, :] = jnp.broadcast_to(
                ref[i:i + 1, :], (LANES, LANES)).T

    def shrink(it):
        for i in range(vrows):
            SRC1[it, i:i + 1, :] = jnp.sum(
                RS[i * LANES:(i + 1) * LANES, :].T, axis=0, keepdims=True)

    def stage1(it):
        shrink(it)

        def one(d, _):
            send(SRC1.at[it], AR1.at[it, d - 1], a1s.at[it], a1r.at[it], peer1(d))
            return 0

        lax.fori_loop(1, n1, one, 0)

    def stage2(it):
        arrived(AR1.at[it], a1r.at[it])
        total = SRC1[it]
        for d in range(n1 - 1):
            total = total + AR1[it, d]
        SRC2[it] = total

        def one(d, _):
            send(SRC2.at[it], AR2.at[it, d - 1], a2s.at[it], a2r.at[it], peer2(d))
            return 0

        lax.fori_loop(1, n2, one, 0)

    def finish(it):
        arrived(AR2.at[it], a2r.at[it])
        total = SRC2[it]
        for d in range(n2 - 1):
            total = total + AR2[it, d]
        MSRC[it] = 1.0 / total

    def column_scales(slot, cols, width):
        def body(i, acc):
            for k in range(4):
                rows = pl.ds(pl.multiple_of(i * 32 + k * 8, 8), 8)
                acc = acc + AB[0, rows, cols] * across(COL[slot, rows, :], width)
            return acc

        acc = lax.fori_loop(0, B // 32, body, jnp.zeros((8, width), F32))
        u = 1.0 / jnp.sum(acc, axis=0, keepdims=True)
        U[:, cols] = u
        return u

    def row_parts(u):
        ub = jnp.broadcast_to(u, (8, PC))

        def body(i, _):
            for k in range(4):
                rows = pl.ds(pl.multiple_of(i * 32 + k * 8, 8), 8)
                m = AB[0, rows, :] * ub
                acc = m[:, :LANES]
                for l in range(1, PC // LANES):
                    acc = acc + m[:, l * LANES:(l + 1) * LANES]
                RS[rows, :] = acc
            return 0

        lax.fori_loop(0, B // 32, body, 0)

    fwd_half = my_half

    def forward():
        arrived(EB.at[1 - role, my_half], e_recv.at[1])
        send(EB.at[1 - role, fwd_half], EB.at[1 - role, fwd_half], e_send.at[2], e_recv.at[2], other_core)

    def other_role():
        arrived(EB.at[1 - role, my_half], e_recv.at[2])
        arrived(WB.at[1 - role, :, gcols], w_recv.at[0])
        for i in range(B // TILE):
            ET[:, i * TILE:(i + 1) * TILE] = EB[1, i * TILE:(i + 1) * TILE, :].T

        def tile(j, _):
            cols = pl.ds(pl.multiple_of(role * PG + j * TILE, TILE), TILE)
            s = jnp.dot(EB[1 - role], WB[1 - role, :, cols], preferred_element_type=F32)
            AB[1 - role, :, cols] = jnp.exp(s * other_scale)
            return 0

        lax.fori_loop(0, PG // TILE, tile, 0)

    own_e.wait()
    own_w.wait()
    arrived(EB.at[role, my_half], e_recv.at[0])
    RS[...] = jnp.zeros_like(RS)

    def own_tile(j, _):
        cols = pl.ds(pl.multiple_of(j * TILE, TILE), TILE)
        s = jnp.dot(EB[role], WB[role, :, cols], preferred_element_type=F32)
        a = jnp.exp(s * scale)
        AB[role, :, cols] = a
        u = jnp.where(teacher, 1.0 / jnp.sum(a, axis=0, keepdims=True), 1.0)
        acc = RS[...]
        for l in range(TILE // LANES):
            acc = acc + a[:, l * LANES:(l + 1) * LANES] * u[:, l * LANES:(l + 1) * LANES]
        RS[...] = acc
        return 0

    lax.fori_loop(0, PC // TILE, own_tile, 0)
    stage1(0)
    stage2(0)
    finish(0)

    @pl.when(teacher)
    def _():
        expand(MSRC.at[0], R1)
        row_parts(column_scales(R1, slice(None), PC))
        stage1(1)
        forward()
        stage2(1)
        finish(1)
        send(MSRC.at[1], MSG.at[1], m_send.at[1], m_recv.at[1], partner)
        expand(MSRC.at[1], R2)
        row_parts(column_scales(R2, slice(None), PC))
        stage1(2)
        stage2(2)
        other_role()
        arrived(MSG.at[0], m_recv.at[0])
        expand(MSG.at[0], SINV)
        finish(2)
        send(MSRC.at[2], MSG.at[2], m_send.at[2], m_recv.at[2], partner)
        expand(MSRC.at[2], R3)

    @pl.when(jnp.logical_not(teacher))
    def _():
        send(MSRC.at[0], MSG.at[0], m_send.at[0], m_recv.at[0], partner)
        expand(MSRC.at[0], SINV)
        forward()
        other_role()
        arrived(MSG.at[1], m_recv.at[1])
        expand(MSG.at[1], R2)
        column_scales(R2, gcols, PG)
        arrived(MSG.at[2], m_recv.at[2])
        expand(MSG.at[2], R3)

    xrows = half // nx

    def block(h, xb):
        start = pl.multiple_of(h * half + xb * xrows, xrows)

        def body(i, _):
            rows = pl.ds(pl.multiple_of(start + i * 16, 16), 16)
            t = AB[0, rows, gcols] * U[:, gcols] * across(COL[R3, rows, :], PG)
            s = AB[1, rows, gcols] * across(COL[SINV, rows, :], PG)
            G[rows, :] = ((s - t.astype(BF16).astype(F32)) * 10.0).astype(BF16)
            return 0

        lax.fori_loop(0, xrows // 16, body, 0)
        EGP[h, pl.ds(pl.multiple_of(xb * xrows, xrows), xrows), :] = lax.dot_general(
            G[pl.ds(start, xrows), :], WB[1, :, gcols], (((1,), (1,)), ((), ())),
            preferred_element_type=F32)

    def chunk(d):
        xb = (x + 1 + d) % nx
        return xb, pl.ds(pl.multiple_of(xb * xrows, xrows), xrows)

    def core_sum(d):
        xb, rows = chunk(d)
        arrived(RC.at[rows], c_recv.at[d])
        EGP[c, rows, :] = EGP[c, rows, :] + RC[rows, :]

    def x_step(d, _):
        xb, rows = chunk(d)
        block(1 - c, xb)
        send(EGP.at[1 - c, rows], RC.at[rows], c_send.at[d], c_recv.at[d], other_core)
        block(c, xb)
        core_sum(d)

        @pl.when(d < nx - 1)
        def _():
            send(EGP.at[c, rows], RX.at[d], x_send.at[d], x_recv.at[d], at(role, xb, yh, z, c))
        return 0

    lax.fori_loop(0, nx, x_step, 0)

    my_q = 2 * c + role

    def wg_tile(j, _):
        cols = pl.ds(pl.multiple_of(j * TILE, TILE), TILE)
        WGB[:, cols] = jnp.dot(ET[...], G[:, cols], preferred_element_type=F32).astype(BF16)
        dst = wg_out.at[0, 0, :, pl.ds(pl.multiple_of(c * PC + role * PG + j * TILE, TILE), TILE)]
        for d in range(1, 4):
            q = (my_q + d) % 4
            src = WGB.at[pl.ds(pl.multiple_of(q * quarter, quarter), quarter), cols]
            send(src, dst, g_send.at[0], g_recv.at[0], at(q % 2, x, yh, z, q // 2))
        return 0

    lax.fori_loop(0, PG // TILE, wg_tile, 0)
    mine = pltpu.make_async_copy(
        WGB.at[pl.ds(pl.multiple_of(my_q * quarter, quarter), quarter)],
        wg_out.at[0, 0, :, pl.ds(pl.multiple_of(c * PC + role * PG, PG), PG)], g_loc.at[0])
    mine.start()

    _, own_rows = chunk(nx - 1)
    total = EGP[c, own_rows, :]
    for d in range(nx - 1):
        arrived(RX.at[d], x_recv.at[d])
        total = total + RX[d]
    S1[...] = total.reshape(S1.shape)
    if nz > 1:
        for d in range(1, nz):
            zz = (z + d) % nz
            send(S1.at[:, zz], RZ.at[d - 1], z_send.at[0], z_recv.at[0], at(role, x, yh, zz, c))
        arrived(RZ, z_recv.at[0])
    part = S1[:, z]
    for d in range(nz - 1):
        part = part + RZ[d]
    for g in range(2):
        S2[g] = part[:, :, g * (D // 2):(g + 1) * (D // 2)]
    my_y = 2 * yh + role
    for d in range(1, 2 * nyh):
        j = (my_y + d) % (2 * nyh)
        send(S2.at[j % 2, j // 2], RY.at[d - 1], y_send.at[0], y_recv.at[0], at(j % 2, x, j // 2, z, c))
    arrived(RY, y_recv.at[0])
    out = S2[role, yh]
    for d in range(2 * nyh - 1):
        out = out + RY[d]
    eg_out[...] = out

    e_core.wait_send()
    e_wrap.wait_send()
    arrived(EB.at[role, my_half], e_send.at[2])
    w_swap.wait_send()

    def sent(it):
        arrived(AR1.at[it], a1s.at[it])
        arrived(AR2.at[it], a2s.at[it])

    sent(0)

    @pl.when(teacher)
    def _():
        sent(1)
        sent(2)
        arrived(MSG.at[1], m_send.at[1])
        arrived(MSG.at[2], m_send.at[2])

    @pl.when(jnp.logical_not(teacher))
    def _():
        arrived(MSG.at[0], m_send.at[0])

    for d in range(nx):
        arrived(RC.at[pl.ds(0, xrows)], c_send.at[d])
    for d in range(nx - 1):
        arrived(RX.at[d], x_send.at[d])
    if nz > 1:
        arrived(RZ, z_send.at[0])
    arrived(RY, y_send.at[0])
    three = wg_out.at[0, 0, :, pl.ds(0, 3 * PG)]
    arrived(three, g_recv.at[0])
    arrived(three, g_send.at[0])
    mine.wait()


def p_count(chips):
    return chips[0] * chips[1] * chips[2]


def solution(mesh):
    chips = CHIPS[mesh.shape["proto"]]
    nx, nyh, nz = chips

    def per_device(emb, wgt):
        half, D = emb.shape[1:]
        B, PC = 2 * half, wgt.shape[2] // 2
        PG = PC // 2
        vrows, owned, xrows = B // LANES, half // p_count(chips), half // nx
        dma = pltpu.SemaphoreType.DMA
        wg, eg = pl.pallas_call(
            functools.partial(kernel, chips),
            name="head_step",
            out_shape=(
                jax.ShapeDtypeStruct((1, 1, D // 4, 2 * PC), BF16),
                jax.ShapeDtypeStruct((owned, D // 2), F32),
            ),
            in_specs=[pl.BlockSpec(memory_space=pl.ANY)] * 2,
            out_specs=(pl.BlockSpec(memory_space=pl.ANY), pl.BlockSpec(memory_space=pltpu.VMEM)),
            scratch_shapes=[
                pltpu.VMEM((2, B, D), BF16),
                pltpu.VMEM((2, D, PC), BF16),
                pltpu.VMEM((2, B, PC), F32),
                pltpu.VMEM((B, PG), BF16),
                pltpu.VMEM((D, B), BF16),
                pltpu.VMEM((1, PC), F32),
                pltpu.VMEM((B, LANES), F32),
                pltpu.VMEM((4, B, LANES), F32),
                pltpu.VMEM((3, vrows, LANES), F32),
                pltpu.VMEM((3, vrows, LANES), F32),
                pltpu.VMEM((3, 2 * nz - 1, vrows, LANES), F32),
                pltpu.VMEM((3, nx * nyh - 1, vrows, LANES), F32),
                pltpu.VMEM((3, vrows, LANES), F32),
                pltpu.VMEM((3, vrows, LANES), F32),
                pltpu.VMEM((2, half, D), F32),
                pltpu.VMEM((half, D), F32),
                pltpu.VMEM((max(nx - 1, 1), xrows, D), F32),
                pltpu.VMEM((nyh, nz, owned, D), F32),
                pltpu.VMEM((max(nz - 1, 1), nyh, owned, D), F32),
                pltpu.VMEM((2, nyh, owned, D // 2), F32),
                pltpu.VMEM((2 * nyh - 1, owned, D // 2), F32),
                pltpu.VMEM((D, PG), BF16),
                dma((2,)), dma((3,)), dma((3,)), dma((1,)), dma((1,)),
                dma((3,)), dma((3,)), dma((3,)), dma((3,)), dma((3,)), dma((3,)),
                dma((nx,)), dma((nx,)), dma((nx,)), dma((nx,)),
                dma((1,)), dma((1,)), dma((1,)), dma((1,)), dma((1,)), dma((1,)), dma((1,)),
            ],
            compiler_params=pltpu.CompilerParams(
                collective_id=0, has_side_effects=True, vmem_limit_bytes=56 * 1024 * 1024),
            cost_estimate=pl.CostEstimate(
                flops=2 * B * D * PG * 5, bytes_accessed=8 * D * PC, transcendentals=3 * B * PG),
        )(emb, wgt)
        return wg, eg.astype(BF16)[None]

    return jax.shard_map(
        per_device,
        mesh=mesh,
        in_specs=(P("role", "crop", None), P("role", None, "proto")),
        out_specs=(P("crop", "role", None, "proto"), P("crop", "proto", "role")),
        check_vma=False,
    )
```

time: 284 us -> 95.2 us (0.34)
  waiting for transfers between devices: 128 us -> 0 us
  Pallas kernels: 0 us -> 89.5 us
  blocking collectives: 72.6 us -> 0 us
  other arithmetic: 45.3 us -> 1.29 us
  starting transfers between devices: 21.3 us -> 0 us
  matrix products: 7.98 us -> 0 us
  local copies, waits for them, and re-layouts: 6.66 us -> 2.29 us
    ppermute x3 -> x0, waiting for transfers between devices: 102 us -> none  [passed_along(): lax.ppermute(value, axis, [(source, source + steps) for source in range(f...]
    pallas_call x0 -> x1, Pallas kernels: none -> 89.5 us  [per_device(): pl.pallas_call(functools.partial(kernel, chips), name='head_step', out_sh...]
    all_to_all x6 -> x0, blocking collectives: 72.6 us -> none  [sent_to_all(): return lax.all_to_all(copies, axis, split_axis=0, concat_axis=0, tiled=True)]
    reduce_sum x13 -> x0, other arithmetic: 28.5 us -> none  [the longest x3 13.8 us: per_device(): jnp.sum(jnp.exp(unnormalized_array + column_shift[None, :]), axis=1)]
    all_to_all x2 -> x0, waiting for transfers between devices: 26.6 us -> none  [sum_at_owner(): blocks = lax.all_to_all(in_blocks(x, dim, peers), axis, 0, 0, tiled=True)]
    all_to_all x2 -> x0, starting transfers between devices: 14.5 us -> none  [sum_at_owner(): blocks = lax.all_to_all(in_blocks(x, dim, peers), axis, 0, 0, tiled=True)]
    convert_element_type x2 -> x0, other arithmetic: 13.9 us -> none  [the longest x1 7.06 us: per_device(): ((tempered - received_parts.astype(jnp.float32)) / 0.1).astype(jnp.bfloat16)]
    dot_general x1 -> x0, matrix products: 7.98 us -> none  [per_device(): jnp.dot(own_embed, own_weight, preferred_element_type=jnp.float32)]
  transfers between devices with their start and end apart: 5 -> 0, of which waited for: 4 -> 0; matrix products, arithmetic and copies ran while one was open for 3% -> 0% of each run, Pallas kernels for 0% -> 0%
where the time goes in v1:
time: 95.2 us; the launch traced here: 93.7 us
  Pallas kernels  89.5 us (94%)
  local copies, waits for them, and re-layouts  2.29 us (2%)
  other arithmetic  1.29 us (1%)
    pallas_call x1, Pallas kernels, per_device(): pl.pallas_call(functools.partial(kernel, chips), name='head_step', out_sh...  89.5 us
    unnamed x1, local copies, waits for them, and re-layouts  2.29 us

profile of v1, /device:TPU:1, one launch (start us, length us, event | category | flops | bytes accessed | tf_op | source)
XLA Modules:
  0.0 93.7 jit_solution(12248412802592406103)
XLA Ops:
  0.6 89.5 %head_step.1 = (bf16[1,1,128,4096]{3,2,1,0:T(8,128)(2,1)}, f32[8,256]{1,0:T(8,128)}) custom-call(bf16[1,512,512]{2,1,0:T(8,128)(2,1)} %emb.1, bf16[1,512,4096]{2,1,0:T(8,128)(2,1)} %wgt.1), custom_call_target="tpu_custom_call" | custom-call | flops 5368709120 | bytes 8388608 | tf_op jit(solution)/shard_map/head_step/pallas_call | solution.py:372
  90.1 1.3 %convert_bitcast_fusion = bf16[1,8,256]{2,1,0:T(8,128)(2,1)} fusion(f32[8,256]{1,0:T(8,128)} %get-tuple-element.5), kind=kLoop, calls=%fused_computation | loop fusion | flops 2048 | bytes 12288 | tf_op jit(solution)/shard_map/broadcast_in_dim | solution.py:414
  91.4 2.3 %copy.5 = bf16[1,1,128,4096]{3,2,1,0:T(8,128)(2,1)} copy(bf16[1,1,128,4096]{3,2,1,0:T(8,128)(2,1)} %get-tuple-element.8) | data formatting | bytes 2097152

commit v2 on v0

v2 whole, which is shorter than its diff:
```python
import functools

import jax
import jax.numpy as jnp
from jax import lax
from jax.experimental import pallas as pl
from jax.experimental.pallas import tpu as pltpu
from jax.sharding import PartitionSpec as P

F32 = jnp.float32
BF16 = jnp.bfloat16
MESH = pl.DeviceIdType.MESH
LANES = 128
TILE = 256
CHIPS = {64: (4, 2, 8), 8: (2, 2, 2), 4: (2, 2, 1)}
BATCHES = (5, 6, 5)


def across(column, width):
    return jnp.concatenate([column] * (width // LANES), axis=1)


def far_first(n):
    return sorted(range(1, n), key=lambda m: -max(min(abs(a - (a ^ m)), n - abs(a - (a ^ m))) for a in range(n)))


def kernel(chips, emb, wgt, wg_out, eg_out,
           EB, WO, WX, KC, AB, G, ET, WT, PCS, PCR, UT, UG, RS, COLR, COLS, COL3,
           SRC1, SRC2, AR1, AR2, AR2S, RV, SV, R3V, EGP, RC, RX, S1, RZ, S2, RY, WGB,
           loc, w_loc, e_send, e_recv, w_send, w_recv, p_send, p_recv, a1s, a1r, a2s, a2r, b_send, b_recv,
           u_send, u_recv, v_send, v_recv, r_send, r_recv, c_send, c_recv, x_send, x_recv,
           z_send, z_recv, y_send, y_recv, g_send, g_recv, g_loc):
    nx, nyh, nz = chips
    role, p, c = (lax.axis_index(a) for a in ("role", "proto", "crop"))
    x, yh, z = p // (nyh * nz), (p // nz) % nyh, p % nz
    teacher = role == 0
    student = role == 1
    half, D = emb.shape[1], emb.shape[2]
    B = 2 * half
    PB = wgt.shape[2]
    PC, PG = PB // 2, PB // 4
    vrows = half // LANES
    crows, grows = PC // LANES, PG // LANES
    quarter = D // 4

    def at(mr=0, mx=0, my=0, mz=0, mc=0):
        return {"role": role ^ mr, "proto": p ^ ((mx * nyh + my) * nz + mz), "crop": c ^ mc}

    def send(src, dst, s, r, to):
        pltpu.make_async_remote_copy(
            src_ref=src, dst_ref=dst, send_sem=s, recv_sem=r, device_id=to, device_id_type=MESH).start()

    def arrived(ref, sem):
        pltpu.make_async_copy(ref, ref, sem).wait()

    z_peers = far_first(nz)
    x_peers = far_first(nx)
    xy_peers = sorted(range(1, nx * nyh), key=lambda m: -((m // nyh in (1, 3)) + 2 * (m // nyh == 2) + 2 * (m % nyh)))

    barrier = pltpu.get_barrier_semaphore()
    greeted = [at(mz=m) for m in z_peers] + [at(mx=m // nyh, my=m % nyh) for m in xy_peers]
    greeted += [at(mr=1, mx=m // nyh, my=m % nyh) for m in range(nx * nyh)] + [at(mc=1), at(mr=1, mc=1)]
    for to in greeted:
        pl.semaphore_signal(barrier, inc=1, device_id=to, device_id_type=MESH)

    my_half = pl.ds(pl.multiple_of(c * half, half), half)
    own_e = pltpu.make_async_copy(emb.at[0], EB.at[role, my_half], loc.at[0])
    own_e.start()
    own_w = []
    for k in range(4):
        cols = pl.ds(k * PG, PG)
        own_w.append(pltpu.make_async_copy(wgt.at[0, :, cols], WO.at[:, cols], w_loc.at[k]))
        own_w[-1].start()

    inv_t, inv_s = 1.0 / 0.07, 1.0 / 0.1
    scale = jnp.where(teacher, inv_t, inv_s).astype(F32)

    own_e.wait()
    for k in range(4):
        own_w[k].wait()

        def own_tile(j, _, k=k):
            cols = pl.ds(pl.multiple_of(k * PG + j * TILE, TILE), TILE)
            s = jnp.dot(EB[role, my_half, :], WO[:, cols], preferred_element_type=F32)
            a = jnp.exp(s * scale)
            KC[:, cols] = a
            cs = jnp.sum(a, axis=0, keepdims=True)
            for l in range(TILE // LANES):
                PCS[0, k // 2, pl.ds((k % 2) * grows + j * (TILE // LANES) + l, 1), :] = cs[:, l * LANES:(l + 1) * LANES]
            return 0

        lax.fori_loop(0, PG // TILE, own_tile, 0)

    pl.semaphore_wait(barrier, len(greeted))

    g_own = pl.multiple_of(c * PC + role * PG, PG)
    g_away = pl.multiple_of(c * PC + (1 - role) * PG, PG)
    step_rows = D // sum(BATCHES)

    def send_columns(it, h):
        send(PCS.at[it, h], PCR.at[it, h], p_send.at[it, h], p_recv.at[it, h], at(mc=1))

    def send_core():
        send(emb.at[0], EB.at[role, my_half], e_send.at[0], e_recv.at[0], at(mc=1))

    def send_wrap(h):
        rows = pl.ds(h * (half // 2), half // 2)
        there = pl.ds(pl.multiple_of(c * half + h * (half // 2), half // 2), half // 2)
        send(emb.at[0, rows], EB.at[role, there], e_send.at[1], e_recv.at[1], at(mr=1, my=1))

    def send_weights(k):
        for q in range(sum(BATCHES[:k]), sum(BATCHES[:k + 1])):
            rows = pl.ds(q * step_rows, step_rows)
            send(wgt.at[0, rows, pl.ds(g_away, PG)], WX.at[rows, :], w_send.at[0], w_recv.at[0], at(mr=1))

    def expand(vec, ref, first=0):
        for i in range(vrows):
            rows = pl.ds(pl.multiple_of(first + i * LANES, LANES), LANES)
            ref[rows, :] = jnp.broadcast_to(vec[i:i + 1, :], (LANES, LANES)).T

    def column_parts(it, h):
        def body(i, acc):
            for k in range(4):
                rows = pl.ds(pl.multiple_of(i * 32 + k * 8, 8), 8)
                acc = acc + KC[rows, h * PC:(h + 1) * PC] * across(COLR[rows, :], PC)
            return acc

        acc = lax.fori_loop(0, half // 32, body, jnp.zeros((8, PC), F32))
        cs = jnp.sum(acc, axis=0, keepdims=True)
        for l in range(crows):
            PCS[it, h, l:l + 1, :] = cs[:, l * LANES:(l + 1) * LANES]
        send_columns(it, h)

    def column_scales(it, h):
        arrived(PCR.at[it, h], p_recv.at[it, h])
        UT[h] = 1.0 / (PCS[it, h] + PCR[it, h])

    def row_parts(h):
        ub = jnp.concatenate(
            [jnp.broadcast_to(UT[h, l:l + 1, :], (8, LANES)) for l in range(crows)], axis=1)

        def body(i, _):
            for k in range(4):
                rows = pl.ds(pl.multiple_of(i * 32 + k * 8, 8), 8)
                m = KC[rows, h * PC:(h + 1) * PC] * ub
                parts = [m[:, l * LANES:(l + 1) * LANES] for l in range(crows)]
                while len(parts) > 1:
                    parts = [a + b for a, b in zip(parts[::2], parts[1::2])]
                RS[rows, :] = parts[0] if h == 0 else RS[rows, :] + parts[0]
            return 0

        lax.fori_loop(0, half // 32, body, 0)

    def stage1(it):
        for i in range(vrows):
            SRC1[it, i:i + 1, :] = jnp.sum(RS[i * LANES:(i + 1) * LANES, :].T, axis=0, keepdims=True)
        for m in z_peers:
            send(SRC1.at[it], AR1.at[it, m - 1], a1s.at[it], a1r.at[it], at(mz=m))

    def stage2(it):
        total = SRC1[it]
        if nz > 1:
            arrived(AR1.at[it], a1r.at[it])
            for m in range(nz - 1):
                total = total + AR1[it, m]
        SRC2[it] = total
        for m in xy_peers:
            send(SRC2.at[it], AR2.at[it, m - 1], a2s.at[it], a2r.at[it], at(mx=m // nyh, my=m % nyh))
        if it == 2:
            for m in range(nx * nyh):
                send(SRC2.at[it], AR2S.at[m], b_send.at[0], b_recv.at[0], at(mr=1, mx=m // nyh, my=m % nyh))

    def finish(it):
        arrived(AR2.at[it], a2r.at[it])
        total = SRC2[it]
        for m in range(nx * nyh - 1):
            total = total + AR2[it, m]
        return 1.0 / total

    def forward():
        arrived(EB.at[1 - role, my_half], e_recv.at[1])
        send(EB.at[1 - role, my_half], EB.at[1 - role, my_half], e_send.at[2], e_recv.at[2], at(mc=1))

    def exps(which, weights, first, inv, scaled):
        def tile(j, _):
            cols = pl.ds(pl.multiple_of(j * TILE, TILE), TILE)
            w_cols = pl.ds(pl.multiple_of(first + j * TILE, TILE), TILE)
            s = jnp.dot(EB[which], weights[:, w_cols], preferred_element_type=F32)
            a = jnp.exp(s * inv)
            AB[which, :, cols] = a * across(COLS[...], TILE) if scaled else a
            return 0

        lax.fori_loop(0, PG // TILE, tile, 0)

    def scale_targets():
        ub = jnp.concatenate(
            [jnp.broadcast_to(UG[l:l + 1, :], (8, LANES)) for l in range(grows)], axis=1)

        def body(i, _):
            for k in range(4):
                rows = pl.ds(pl.multiple_of(i * 32 + k * 8, 8), 8)
                AB[0, rows, :] = AB[0, rows, :] * ub
            return 0

        lax.fori_loop(0, B // 32, body, 0)

    def turn_student(weights, first):
        for i in range(B // TILE):
            ET[:, i * TILE:(i + 1) * TILE] = EB[1, i * TILE:(i + 1) * TILE, :].T

        def body(i, _):
            rows = pl.ds(pl.multiple_of(i * TILE, TILE), TILE)
            WT[rows, :] = weights[:, pl.ds(pl.multiple_of(first + i * TILE, TILE), TILE)].T
            return 0

        lax.fori_loop(0, PG // TILE, body, 0)

    @pl.when(teacher)
    def _():
        for h in range(2):
            send_columns(0, h)
        send_core()
        send_wrap(0)
        send_wrap(1)
        send_weights(0)
        for h in range(2):
            column_scales(0, h)
            row_parts(h)
        stage1(0)
        arrived(EB.at[role, my_half], e_recv.at[0])
        exps(0, WO, g_own, inv_t, False)
        stage2(0)
        r = finish(0)
        for it in (1, 2):
            expand(r, COLR)
            send_weights(it)
            for h in range(2):
                column_parts(it, h)
            for h in range(2):
                column_scales(it, h)
                row_parts(h)
            stage1(it)
            if it == 1:
                forward()
            else:
                UG[...] = UT[c, 0:grows, :]
                send(UT.at[c, pl.ds(grows, grows)], UG, u_send.at[0], u_recv.at[0], at(mr=1))
                scale_targets()
                arrived(EB.at[1 - role, my_half], e_recv.at[2])
                arrived(WX, w_recv.at[0])
                turn_student(WX, 0)
            stage2(it)
            if it == 2:
                arrived(SV.at[c], v_recv.at[1])
                arrived(SV.at[1 - c], v_recv.at[2])
                for h in range(2):
                    expand(SV[h], COLS, h * half)
                exps(1, WX, 0, inv_s, True)
            r = finish(it)
        R3V[c] = r

    @pl.when(student)
    def _():
        send_core()
        send_wrap(0)
        for k in range(len(BATCHES)):
            send_weights(k)
        for h in range(2):
            UT[h] = jnp.ones((crows, LANES), F32)
            row_parts(h)
        stage1(0)
        stage2(0)
        SV[c] = finish(0)
        send_wrap(1)
        send(SV.at[c], SV.at[c], v_send.at[0], v_recv.at[0], at(mc=1))
        send(SV.at[c], SV.at[c], v_send.at[1], v_recv.at[1], at(mr=1))
        send(SV.at[c], SV.at[c], v_send.at[2], v_recv.at[2], at(mr=1, mc=1))
        forward()
        arrived(SV.at[1 - c], v_recv.at[0])
        for h in range(2):
            expand(SV[h], COLS, h * half)
        arrived(EB.at[role, my_half], e_recv.at[0])
        exps(1, WO, g_own, inv_s, True)
        turn_student(WO, g_own)
        arrived(EB.at[1 - role, my_half], e_recv.at[2])
        arrived(WX, w_recv.at[0])
        exps(0, WX, 0, inv_t, False)
        arrived(UG, u_recv.at[0])
        scale_targets()
        arrived(AR2S, b_recv.at[0])
        total = AR2S[0]
        for m in range(1, nx * nyh):
            total = total + AR2S[m]
        R3V[c] = 1.0 / total

    send(R3V.at[c], R3V.at[c], r_send.at[0], r_recv.at[0], at(mc=1))

    def logit_grads(h):
        expand(R3V[h], COL3, h * half)

        def body(i, _):
            rows = pl.ds(pl.multiple_of(h * half + i * 16, 16), 16)
            t = AB[0, rows, :] * across(COL3[rows, :], PG)
            G[rows, :] = ((AB[1, rows, :] - t.astype(BF16).astype(F32)) * 10.0).astype(BF16)
            return 0

        lax.fori_loop(0, half // 16, body, 0)

    def embed_parts(h):
        rows = pl.ds(pl.multiple_of(h * half, half), half)

        def body(j, _):
            cols = pl.ds(pl.multiple_of(j * TILE, TILE), TILE)
            EGP[h, :, cols] = jnp.dot(G[rows, :], WT[:, cols], preferred_element_type=F32)
            return 0

        lax.fori_loop(0, D // TILE, body, 0)

    xrows = half // nx
    yrows = xrows // nyh
    owned = yrows // nz

    def x_rows(m):
        return pl.ds(pl.multiple_of((x ^ m) * xrows, xrows), xrows)

    logit_grads(c)
    arrived(R3V.at[1 - c], r_recv.at[0])
    logit_grads(1 - c)
    embed_parts(1 - c)
    for m in x_peers + [0]:
        send(EGP.at[1 - c, x_rows(m)], RC.at[x_rows(m)], c_send.at[m], c_recv.at[m], at(mc=1))
    embed_parts(c)
    for h in range(nyh):
        for m in x_peers + [0]:
            rows = pl.ds(pl.multiple_of((x ^ m) * xrows + h * yrows, yrows), yrows)
            if h == 0:
                arrived(RC.at[x_rows(m)], c_recv.at[m])
            EGP[c, rows, :] = EGP[c, rows, :] + RC[rows, :]
            if m:
                send(EGP.at[c, rows], RX.at[h, m - 1], x_send.at[h], x_recv.at[h], at(mx=m))

    my_q = 2 * c + role
    out_first = c * PC + role * PG

    def wg_tile(j, _):
        cols = pl.ds(pl.multiple_of(j * TILE, TILE), TILE)
        WGB[:, cols] = jnp.dot(ET[...], G[:, cols], preferred_element_type=F32).astype(BF16)
        dst = wg_out.at[0, 0, :, pl.ds(pl.multiple_of(out_first + j * TILE, TILE), TILE)]
        for m in (1, 3, 2):
            src = WGB.at[pl.ds(pl.multiple_of((my_q ^ m) * quarter, quarter), quarter), cols]
            send(src, dst, g_send.at[0], g_recv.at[0], at(mr=m % 2, mc=m // 2))
        return 0

    lax.fori_loop(0, PG // TILE, wg_tile, 0)
    mine = pltpu.make_async_copy(
        WGB.at[pl.ds(pl.multiple_of(my_q * quarter, quarter), quarter)],
        wg_out.at[0, 0, :, pl.ds(pl.multiple_of(out_first, PG), PG)], g_loc.at[0])
    mine.start()

    for h in range(nyh):
        rows = pl.ds(pl.multiple_of(x * xrows + h * yrows, yrows), yrows)
        arrived(RX.at[h], x_recv.at[h])
        total = EGP[c, rows, :]
        for m in range(nx - 1):
            total = total + RX[h, m]
        S1[h] = total.reshape(nz, owned, D)
        for m in z_peers:
            send(S1.at[h, z ^ m], RZ.at[h, m - 1], z_send.at[h], z_recv.at[h], at(mz=m))
    for h in range(nyh):
        part = S1[h, z]
        if nz > 1:
            arrived(RZ.at[h], z_recv.at[h])
            for m in range(nz - 1):
                part = part + RZ[h, m]
        for g in range(2):
            S2[g, h] = part[:, g * (D // 2):(g + 1) * (D // 2)]
    for m in range(1, 2 * nyh):
        send(S2.at[role ^ (m % 2), yh ^ (m // 2)], RY.at[m - 1], y_send.at[0], y_recv.at[0],
             at(mr=m % 2, my=m // 2))
    arrived(RY, y_recv.at[0])
    out = S2[role, yh]
    for m in range(2 * nyh - 1):
        out = out + RY[m]
    eg_out[...] = out

    arrived(EB.at[role, my_half], e_send.at[0])
    arrived(EB.at[role, my_half], e_send.at[1])
    arrived(EB.at[role, my_half], e_send.at[2])
    arrived(WX, w_send.at[0])
    arrived(R3V.at[c], r_send.at[0])

    def sent(it):
        if nz > 1:
            arrived(AR1.at[it], a1s.at[it])
        arrived(AR2.at[it], a2s.at[it])

    sent(0)

    @pl.when(teacher)
    def _():
        sent(1)
        sent(2)
        for it in range(3):
            for h in range(2):
                arrived(PCS.at[it, h], p_send.at[it, h])
        arrived(UG, u_send.at[0])
        arrived(AR2S, b_send.at[0])

    @pl.when(student)
    def _():
        for k in range(3):
            arrived(SV.at[0], v_send.at[k])

    for m in range(nx):
        arrived(RC.at[pl.ds(0, xrows)], c_send.at[m])
    for h in range(nyh):
        arrived(RX.at[h], x_send.at[h])
        if nz > 1:
            arrived(RZ.at[h], z_send.at[h])
    arrived(RY, y_send.at[0])
    three = wg_out.at[0, 0, :, pl.ds(0, 3 * PG)]
    arrived(three, g_recv.at[0])
    arrived(three, g_send.at[0])
    mine.wait()


def solution(mesh):
    chips = CHIPS[mesh.shape["proto"]]
    nx, nyh, nz = chips

    def per_device(emb, wgt):
        half, D = emb.shape[1:]
        B, PB = 2 * half, wgt.shape[2]
        PC, PG = PB // 2, PB // 4
        vrows, xrows = half // LANES, half // nx
        yrows = xrows // nyh
        owned = yrows // nz
        dma = lambda *shape: pltpu.SemaphoreType.DMA(shape)
        wg, eg = pl.pallas_call(
            functools.partial(kernel, chips),
            name="head_step",
            out_shape=(
                jax.ShapeDtypeStruct((1, 1, D // 4, PB), BF16),
                jax.ShapeDtypeStruct((owned, D // 2), F32),
            ),
            in_specs=[pl.BlockSpec(memory_space=pl.ANY)] * 2,
            out_specs=(pl.BlockSpec(memory_space=pl.ANY), pl.BlockSpec(memory_space=pltpu.VMEM)),
            scratch_shapes=[
                pltpu.VMEM((2, B, D), BF16),
                pltpu.VMEM((D, PB), BF16),
                pltpu.VMEM((D, PG), BF16),
                pltpu.VMEM((half, PB), F32),
                pltpu.VMEM((2, B, PG), F32),
                pltpu.VMEM((B, PG), BF16),
                pltpu.VMEM((D, B), BF16),
                pltpu.VMEM((PG, D), BF16),
                pltpu.VMEM((3, 2, PC // LANES, LANES), F32),
                pltpu.VMEM((3, 2, PC // LANES, LANES), F32),
                pltpu.VMEM((2, PC // LANES, LANES), F32),
                pltpu.VMEM((PG // LANES, LANES), F32),
                pltpu.VMEM((half, LANES), F32),
                pltpu.VMEM((half, LANES), F32),
                pltpu.VMEM((B, LANES), F32),
                pltpu.VMEM((B, LANES), F32),
                pltpu.VMEM((3, vrows, LANES), F32),
                pltpu.VMEM((3, vrows, LANES), F32),
                pltpu.VMEM((3, max(nz - 1, 1), vrows, LANES), F32),
                pltpu.VMEM((3, nx * nyh - 1, vrows, LANES), F32),
                pltpu.VMEM((nx * nyh, vrows, LANES), F32),
                pltpu.VMEM((3, vrows, LANES), F32),
                pltpu.VMEM((2, vrows, LANES), F32),
                pltpu.VMEM((2, vrows, LANES), F32),
                pltpu.VMEM((2, half, D), F32),
                pltpu.VMEM((half, D), F32),
                pltpu.VMEM((nyh, nx - 1, yrows, D), F32),
                pltpu.VMEM((nyh, nz, owned, D), F32),
                pltpu.VMEM((nyh, max(nz - 1, 1), owned, D), F32),
                pltpu.VMEM((2, nyh, owned, D // 2), F32),
                pltpu.VMEM((2 * nyh - 1, owned, D // 2), F32),
                pltpu.VMEM((D, PG), BF16),
                dma(1), dma(4), dma(3), dma(3), dma(1), dma(1), dma(3, 2), dma(3, 2),
                dma(3), dma(3), dma(3), dma(3), dma(1), dma(1),
                dma(1), dma(1), dma(3), dma(3), dma(1), dma(1), dma(nx), dma(nx), dma(nyh), dma(nyh),
                dma(nyh), dma(nyh), dma(1), dma(1), dma(1), dma(1), dma(1),
            ],
            compiler_params=pltpu.CompilerParams(
                collective_id=0, has_side_effects=True, vmem_limit_bytes=56 * 1024 * 1024),
            cost_estimate=pl.CostEstimate(
                flops=2 * B * D * PG * 6, bytes_accessed=2 * D * PB, transcendentals=4 * B * PG),
        )(emb, wgt)
        return wg, eg.astype(BF16)[None]

    return jax.shard_map(
        per_device,
        mesh=mesh,
        in_specs=(P("role", "crop", None), P("role", None, "proto")),
        out_specs=(P("crop", "role", None, "proto"), P("crop", "proto", "role")),
        check_vma=False,
    )
```

time: 284 us -> 93.2 us (0.33)
  waiting for transfers between devices: 128 us -> 0 us
  Pallas kernels: 0 us -> 88.8 us
  blocking collectives: 72.6 us -> 0 us
  other arithmetic: 45.3 us -> 1.29 us
  starting transfers between devices: 21.3 us -> 0 us
  matrix products: 7.98 us -> 0 us
  local copies, waits for them, and re-layouts: 6.66 us -> 2.29 us
    ppermute x3 -> x0, waiting for transfers between devices: 102 us -> none  [passed_along(): lax.ppermute(value, axis, [(source, source + steps) for source in range(f...]
    pallas_call x0 -> x1, Pallas kernels: none -> 88.8 us  [per_device(): pl.pallas_call(functools.partial(kernel, chips), name='head_step', out_sh...]
    all_to_all x6 -> x0, blocking collectives: 72.6 us -> none  [sent_to_all(): return lax.all_to_all(copies, axis, split_axis=0, concat_axis=0, tiled=True)]
    reduce_sum x13 -> x0, other arithmetic: 28.5 us -> none  [the longest x3 13.8 us: per_device(): jnp.sum(jnp.exp(unnormalized_array + column_shift[None, :]), axis=1)]
    all_to_all x2 -> x0, waiting for transfers between devices: 26.6 us -> none  [sum_at_owner(): blocks = lax.all_to_all(in_blocks(x, dim, peers), axis, 0, 0, tiled=True)]
    all_to_all x2 -> x0, starting transfers between devices: 14.5 us -> none  [sum_at_owner(): blocks = lax.all_to_all(in_blocks(x, dim, peers), axis, 0, 0, tiled=True)]
    convert_element_type x2 -> x0, other arithmetic: 13.9 us -> none  [the longest x1 7.06 us: per_device(): ((tempered - received_parts.astype(jnp.float32)) / 0.1).astype(jnp.bfloat16)]
    dot_general x1 -> x0, matrix products: 7.98 us -> none  [per_device(): jnp.dot(own_embed, own_weight, preferred_element_type=jnp.float32)]
  transfers between devices with their start and end apart: 5 -> 0, of which waited for: 4 -> 0; matrix products, arithmetic and copies ran while one was open for 3% -> 0% of each run, Pallas kernels for 0% -> 0%
where the time goes in v2:
time: 93.2 us; the launch traced here: 93.1 us
  Pallas kernels  88.8 us (95%)
  local copies, waits for them, and re-layouts  2.29 us (2%)
  other arithmetic  1.29 us (1%)
    pallas_call x1, Pallas kernels, per_device(): pl.pallas_call(functools.partial(kernel, chips), name='head_step', out_sh...  88.8 us
    unnamed x1, local copies, waits for them, and re-layouts  2.29 us

profile of v2, /device:TPU:1, one launch (start us, length us, event | category | flops | bytes accessed | tf_op | source)
XLA Modules:
  0.0 93.1 jit_solution(5689807977237664310)
XLA Ops:
  0.6 88.8 %head_step.1 = (bf16[1,1,128,4096]{3,2,1,0:T(8,128)(2,1)}, f32[8,256]{1,0:T(8,128)}) custom-call(bf16[1,512,512]{2,1,0:T(8,128)(2,1)} %emb.1, bf16[1,512,4096]{2,1,0:T(8,128)(2,1)} %wgt.1), custom_call_target="tpu_custom_call" | custom-call | flops 6442450944 | bytes 4194304 | tf_op jit(solution)/shard_map/head_step/pallas_call | solution.py:439
  89.5 1.3 %convert_bitcast_fusion = bf16[1,8,256]{2,1,0:T(8,128)(2,1)} fusion(f32[8,256]{1,0:T(8,128)} %get-tuple-element.5), kind=kLoop, calls=%fused_computation | loop fusion | flops 2048 | bytes 12288 | tf_op jit(solution)/shard_map/broadcast_in_dim | solution.py:491
  90.8 2.3 %copy.5 = bf16[1,1,128,4096]{3,2,1,0:T(8,128)(2,1)} copy(bf16[1,1,128,4096]{3,2,1,0:T(8,128)(2,1)} %get-tuple-element.8) | data formatting | bytes 2097152

commit v3 on v2

--- a/solution.py
+++ b/solution.py
@@ -26,7 +26,7 @@
 
 def kernel(chips, emb, wgt, wg_out, eg_out,
            EB, WO, WX, KC, AB, G, ET, WT, PCS, PCR, UT, UG, RS, COLR, COLS, COL3,
-           SRC1, SRC2, AR1, AR2, AR2S, RV, SV, R3V, EGP, RC, RX, S1, RZ, S2, RY, WGB,
+           SRC1, SRC2, AR1, AR2, AR2S, SV, R3V, EGP, RC, RX, S1, RZ, S2, RY, WGB,
            loc, w_loc, e_send, e_recv, w_send, w_recv, p_send, p_recv, a1s, a1r, a2s, a2r, b_send, b_recv,
            u_send, u_recv, v_send, v_recv, r_send, r_recv, c_send, c_recv, x_send, x_recv,
            z_send, z_recv, y_send, y_recv, g_send, g_recv, g_loc):
@@ -221,7 +221,6 @@
             send_columns(0, h)
         send_core()
         send_wrap(0)
-        send_wrap(1)
         send_weights(0)
         for h in range(2):
             column_scales(0, h)
@@ -234,15 +233,15 @@
         for it in (1, 2):
             expand(r, COLR)
             send_weights(it)
+            if it == 1:
+                send_wrap(1)
             for h in range(2):
                 column_parts(it, h)
             for h in range(2):
                 column_scales(it, h)
                 row_parts(h)
             stage1(it)
-            if it == 1:
-                forward()
-            else:
+            if it == 2:
                 UG[...] = UT[c, 0:grows, :]
                 send(UT.at[c, pl.ds(grows, grows)], UG, u_send.at[0], u_recv.at[0], at(mr=1))
                 scale_targets()
@@ -250,7 +249,9 @@
                 arrived(WX, w_recv.at[0])
                 turn_student(WX, 0)
             stage2(it)
-            if it == 2:
+            if it == 1:
+                forward()
+            else:
                 arrived(SV.at[c], v_recv.at[1])
                 arrived(SV.at[1 - c], v_recv.at[2])
                 for h in range(2):
@@ -263,18 +264,19 @@
     def _():
         send_core()
         send_wrap(0)
-        for k in range(len(BATCHES)):
-            send_weights(k)
+        send_wrap(1)
+        send_weights(0)
         for h in range(2):
             UT[h] = jnp.ones((crows, LANES), F32)
             row_parts(h)
         stage1(0)
         stage2(0)
         SV[c] = finish(0)
-        send_wrap(1)
         send(SV.at[c], SV.at[c], v_send.at[0], v_recv.at[0], at(mc=1))
         send(SV.at[c], SV.at[c], v_send.at[1], v_recv.at[1], at(mr=1))
         send(SV.at[c], SV.at[c], v_send.at[2], v_recv.at[2], at(mr=1, mc=1))
+        for k in range(1, len(BATCHES)):
+            send_weights(k)
         forward()
         arrived(SV.at[1 - c], v_recv.at[0])
         for h in range(2):
@@ -467,7 +469,6 @@
                 pltpu.VMEM((3, max(nz - 1, 1), vrows, LANES), F32),
                 pltpu.VMEM((3, nx * nyh - 1, vrows, LANES), F32),
                 pltpu.VMEM((nx * nyh, vrows, LANES), F32),
-                pltpu.VMEM((3, vrows, LANES), F32),
                 pltpu.VMEM((2, vrows, LANES), F32),
                 pltpu.VMEM((2, vrows, LANES), F32),
                 pltpu.VMEM((2, half, D), F32),

time: 93.2 us -> 78.2 us (0.84)
  Pallas kernels: 88.8 us -> 73 us
    pallas_call x1, Pallas kernels: 88.8 us -> 73 us  [per_device(): pl.pallas_call(functools.partial(kernel, chips), name='head_step', out_sh...]
where the time goes in v3:
time: 78.2 us; the launch traced here: 77.2 us
  Pallas kernels  73 us (93%)
  local copies, waits for them, and re-layouts  2.29 us (3%)
  other arithmetic  1.29 us (2%)
    pallas_call x1, Pallas kernels, per_device(): pl.pallas_call(functools.partial(kernel, chips), name='head_step', out_sh...  73 us
    unnamed x1, local copies, waits for them, and re-layouts  2.29 us

profile of v3, /device:TPU:1, one launch (start us, length us, event | category | flops | bytes accessed | tf_op | source)
XLA Modules:
  0.0 77.2 jit_solution(11401793992237804440)
XLA Ops:
  0.6 73.0 %head_step.1 = (bf16[1,1,128,4096]{3,2,1,0:T(8,128)(2,1)}, f32[8,256]{1,0:T(8,128)}) custom-call(bf16[1,512,512]{2,1,0:T(8,128)(2,1)} %emb.1, bf16[1,512,4096]{2,1,0:T(8,128)(2,1)} %wgt.1), custom_call_target="tpu_custom_call" | custom-call | flops 6442450944 | bytes 4194304 | tf_op jit(solution)/shard_map/head_step/pallas_call | solution.py:441
  73.6 1.3 %convert_bitcast_fusion = bf16[1,8,256]{2,1,0:T(8,128)(2,1)} fusion(f32[8,256]{1,0:T(8,128)} %get-tuple-element.5), kind=kLoop, calls=%fused_computation | loop fusion | flops 2048 | bytes 12288 | tf_op jit(solution)/shard_map/broadcast_in_dim | solution.py:492
  74.9 2.3 %copy.5 = bf16[1,1,128,4096]{3,2,1,0:T(8,128)(2,1)} copy(bf16[1,1,128,4096]{3,2,1,0:T(8,128)(2,1)} %get-tuple-element.8) | data formatting | bytes 2097152

commit v4 on v3

--- a/solution.py
+++ b/solution.py
@@ -26,10 +26,10 @@
 
 def kernel(chips, emb, wgt, wg_out, eg_out,
            EB, WO, WX, KC, AB, G, ET, WT, PCS, PCR, UT, UG, RS, COLR, COLS, COL3,
-           SRC1, SRC2, AR1, AR2, AR2S, SV, R3V, EGP, RC, RX, S1, RZ, S2, RY, WGB,
+           SRC1, ALL, SRC2, AR1, AR2, AR2S, SV, R3V, EGP, RC, RX, S1, RZ, WGB,
            loc, w_loc, e_send, e_recv, w_send, w_recv, p_send, p_recv, a1s, a1r, a2s, a2r, b_send, b_recv,
            u_send, u_recv, v_send, v_recv, r_send, r_recv, c_send, c_recv, x_send, x_recv,
-           z_send, z_recv, y_send, y_recv, g_send, g_recv, g_loc):
+           z_send, z_recv, g_send, g_recv, g_loc):
     nx, nyh, nz = chips
     role, p, c = (lax.axis_index(a) for a in ("role", "proto", "crop"))
     x, yh, z = p // (nyh * nz), (p // nz) % nyh, p % nz
@@ -55,6 +55,13 @@
 
     z_peers = far_first(nz)
     x_peers = far_first(nx)
+    def hops(m):
+        far = 0
+        for n, k in ((nx, m // (nyh * nz)), (nz, m % nz)):
+            far += max(min(abs(a - (a ^ k)), n - abs(a - (a ^ k))) for a in range(n))
+        return far + 2 * ((m // nz) % nyh)
+
+    all_peers = sorted(range(1, nx * nyh * nz), key=lambda m: -hops(m))
     xy_peers = sorted(range(1, nx * nyh), key=lambda m: -((m // nyh in (1, 3)) + 2 * (m // nyh == 2) + 2 * (m % nyh)))
 
     barrier = pltpu.get_barrier_semaphore()
@@ -154,8 +161,8 @@
     def stage1(it):
         for i in range(vrows):
             SRC1[it, i:i + 1, :] = jnp.sum(RS[i * LANES:(i + 1) * LANES, :].T, axis=0, keepdims=True)
-        for m in z_peers:
-            send(SRC1.at[it], AR1.at[it, m - 1], a1s.at[it], a1r.at[it], at(mz=m))
+        for m in all_peers if it == 1 else z_peers:
+            send(SRC1.at[it], ALL.at[m - 1] if it == 1 else AR1.at[it, m - 1], a1s.at[it], a1r.at[it], at(mz=m))
 
     def stage2(it):
         total = SRC1[it]
@@ -171,11 +178,15 @@
                 send(SRC2.at[it], AR2S.at[m], b_send.at[0], b_recv.at[0], at(mr=1, mx=m // nyh, my=m % nyh))
 
     def finish(it):
-        arrived(AR2.at[it], a2r.at[it])
-        total = SRC2[it]
-        for m in range(nx * nyh - 1):
-            total = total + AR2[it, m]
-        return 1.0 / total
+        if it == 1:
+            arrived(ALL, a1r.at[it])
+            parts = [SRC1[it]] + [ALL[m] for m in range(nx * nyh * nz - 1)]
+        else:
+            arrived(AR2.at[it], a2r.at[it])
+            parts = [SRC2[it]] + [AR2[it, m] for m in range(nx * nyh - 1)]
+        while len(parts) > 1:
+            parts = [a + b for a, b in zip(parts[::2], parts[1::2])]
+        return 1.0 / parts[0]
 
     def forward():
         arrived(EB.at[1 - role, my_half], e_recv.at[1])
@@ -248,10 +259,10 @@
                 arrived(EB.at[1 - role, my_half], e_recv.at[2])
                 arrived(WX, w_recv.at[0])
                 turn_student(WX, 0)
-            stage2(it)
             if it == 1:
                 forward()
             else:
+                stage2(it)
                 arrived(SV.at[c], v_recv.at[1])
                 arrived(SV.at[1 - c], v_recv.at[2])
                 for h in range(2):
@@ -297,49 +308,71 @@
 
     send(R3V.at[c], R3V.at[c], r_send.at[0], r_recv.at[0], at(mc=1))
 
-    def logit_grads(h):
-        expand(R3V[h], COL3, h * half)
-
-        def body(i, _):
-            rows = pl.ds(pl.multiple_of(h * half + i * 16, 16), 16)
-            t = AB[0, rows, :] * across(COL3[rows, :], PG)
-            G[rows, :] = ((AB[1, rows, :] - t.astype(BF16).astype(F32)) * 10.0).astype(BF16)
-            return 0
-
-        lax.fori_loop(0, half // 16, body, 0)
-
-    def embed_parts(h):
-        rows = pl.ds(pl.multiple_of(h * half, half), half)
-
-        def body(j, _):
-            cols = pl.ds(pl.multiple_of(j * TILE, TILE), TILE)
-            EGP[h, :, cols] = jnp.dot(G[rows, :], WT[:, cols], preferred_element_type=F32)
-            return 0
-
-        lax.fori_loop(0, D // TILE, body, 0)
-
     xrows = half // nx
     yrows = xrows // nyh
     owned = yrows // nz
+    side = half // 2
+    blocks = nx // 2
+
+    def side_rows(h, far):
+        return pl.multiple_of(h * half + ((x // blocks) ^ far) * side, side)
+
+    def logit_grads(h, far):
+        def body(i, _):
+            rows = pl.ds(pl.multiple_of(side_rows(h, far) + i * 16, 16), 16)
+            t = AB[0, rows, :] * across(COL3[rows, :], PG)
+            G[rows, :] = ((AB[1, rows, :] - t.astype(BF16).astype(F32)) * 10.0).astype(BF16)
+            return 0
+
+        lax.fori_loop(0, side // 16, body, 0)
+
+    def embed_parts(h, far):
+        rows = pl.ds(side_rows(h, far), side)
+        local = pl.ds(pl.multiple_of(((x // blocks) ^ far) * side, side), side)
+
+        def body(j, _):
+            cols = pl.ds(pl.multiple_of(j * TILE, TILE), TILE)
+            EGP[h, local, cols] = jnp.dot(G[rows, :], WT[:, cols], preferred_element_type=F32)
+            return 0
+
+        lax.fori_loop(0, D // TILE, body, 0)
 
     def x_rows(m):
         return pl.ds(pl.multiple_of((x ^ m) * xrows, xrows), xrows)
 
-    logit_grads(c)
-    arrived(R3V.at[1 - c], r_recv.at[0])
-    logit_grads(1 - c)
-    embed_parts(1 - c)
-    for m in x_peers + [0]:
-        send(EGP.at[1 - c, x_rows(m)], RC.at[x_rows(m)], c_send.at[m], c_recv.at[m], at(mc=1))
-    embed_parts(c)
-    for h in range(nyh):
-        for m in x_peers + [0]:
+    far_side = list(range(blocks, nx))
+    near_side = list(range(blocks - 1, -1, -1))
+
+    def send_core_parts(masks):
+        for m in masks:
+            send(EGP.at[1 - c, x_rows(m)], RC.at[x_rows(m)], c_send.at[m], c_recv.at[m], at(mc=1))
+
+    def send_x_parts(h, masks):
+        for m in masks:
             rows = pl.ds(pl.multiple_of((x ^ m) * xrows + h * yrows, yrows), yrows)
             if h == 0:
                 arrived(RC.at[x_rows(m)], c_recv.at[m])
             EGP[c, rows, :] = EGP[c, rows, :] + RC[rows, :]
             if m:
                 send(EGP.at[c, rows], RX.at[h, m - 1], x_send.at[h], x_recv.at[h], at(mx=m))
+
+    expand(R3V[c], COL3, c * half)
+    logit_grads(c, 1)
+    arrived(R3V.at[1 - c], r_recv.at[0])
+    expand(R3V[1 - c], COL3, (1 - c) * half)
+    logit_grads(1 - c, 1)
+    embed_parts(1 - c, 1)
+    send_core_parts(far_side)
+    embed_parts(c, 1)
+    logit_grads(1 - c, 0)
+    embed_parts(1 - c, 0)
+    send_core_parts(near_side)
+    send_x_parts(0, far_side)
+    logit_grads(c, 0)
+    embed_parts(c, 0)
+    send_x_parts(0, near_side)
+    for h in range(1, nyh):
+        send_x_parts(h, far_side + near_side)
 
     my_q = 2 * c + role
     out_first = c * PC + role * PG
@@ -366,24 +399,26 @@
         for m in range(nx - 1):
             total = total + RX[h, m]
         S1[h] = total.reshape(nz, owned, D)
-        for m in z_peers:
-            send(S1.at[h, z ^ m], RZ.at[h, m - 1], z_send.at[h], z_recv.at[h], at(mz=m))
-    for h in range(nyh):
-        part = S1[h, z]
-        if nz > 1:
-            arrived(RZ.at[h], z_recv.at[h])
-            for m in range(nz - 1):
-                part = part + RZ[h, m]
-        for g in range(2):
-            S2[g, h] = part[:, g * (D // 2):(g + 1) * (D // 2)]
-    for m in range(1, 2 * nyh):
-        send(S2.at[role ^ (m % 2), yh ^ (m // 2)], RY.at[m - 1], y_send.at[0], y_recv.at[0],
-             at(mr=m % 2, my=m // 2))
-    arrived(RY, y_recv.at[0])
-    out = S2[role, yh]
-    for m in range(2 * nyh - 1):
-        out = out + RY[m]
-    eg_out[...] = out
+        my = yh ^ h
+        for mz in z_peers + [0]:
+            for mr in (1, 0):
+                src = S1.at[h, z ^ mz, :, pl.ds(pl.multiple_of((role ^ mr) * (D // 2), D // 2), D // 2)]
+                place = RZ.at[(my * 2 + mr) * nz + mz]
+
+                def give(src=src, place=place, mr=mr, mz=mz):
+                    send(src, place, z_send.at[0], z_recv.at[0], at(mr=mr, my=my, mz=mz))
+
+                if mr or mz:
+                    give()
+                else:
+                    pl.when(my != 0)(give)
+    last = RZ.at[pl.ds(1, 2 * nyh * nz - 1)]
+    arrived(last, z_recv.at[0])
+    parts = [S1[yh, z, :, pl.ds(pl.multiple_of(role * (D // 2), D // 2), D // 2)]]
+    parts += [RZ[m] for m in range(1, 2 * nyh * nz)]
+    while len(parts) > 1:
+        parts = [a + b for a, b in zip(parts[::2], parts[1::2])]
+    eg_out[...] = parts[0]
 
     arrived(EB.at[role, my_half], e_send.at[0])
     arrived(EB.at[role, my_half], e_send.at[1])
@@ -400,7 +435,7 @@
 
     @pl.when(teacher)
     def _():
-        sent(1)
+        arrived(ALL, a1s.at[1])
         sent(2)
         for it in range(3):
             for h in range(2):
@@ -417,13 +452,16 @@
         arrived(RC.at[pl.ds(0, xrows)], c_send.at[m])
     for h in range(nyh):
         arrived(RX.at[h], x_send.at[h])
-        if nz > 1:
-            arrived(RZ.at[h], z_send.at[h])
-    arrived(RY, y_send.at[0])
+    arrived(last, z_send.at[0])
     three = wg_out.at[0, 0, :, pl.ds(0, 3 * PG)]
     arrived(three, g_recv.at[0])
     arrived(three, g_send.at[0])
     mine.wait()
+
+
+def finish_outputs(wg, eg, wg_out, eg_out):
+    wg_out[...] = wg[...]
+    eg_out[0] = eg[...].astype(BF16)
 
 
 def solution(mesh):
@@ -465,6 +503,7 @@
                 pltpu.VMEM((B, LANES), F32),
                 pltpu.VMEM((B, LANES), F32),
                 pltpu.VMEM((3, vrows, LANES), F32),
+                pltpu.VMEM((nx * nyh * nz - 1, vrows, LANES), F32),
                 pltpu.VMEM((3, vrows, LANES), F32),
                 pltpu.VMEM((3, max(nz - 1, 1), vrows, LANES), F32),
                 pltpu.VMEM((3, nx * nyh - 1, vrows, LANES), F32),
@@ -475,21 +514,28 @@
                 pltpu.VMEM((half, D), F32),
                 pltpu.VMEM((nyh, nx - 1, yrows, D), F32),
                 pltpu.VMEM((nyh, nz, owned, D), F32),
-                pltpu.VMEM((nyh, max(nz - 1, 1), owned, D), F32),
-                pltpu.VMEM((2, nyh, owned, D // 2), F32),
-                pltpu.VMEM((2 * nyh - 1, owned, D // 2), F32),
+                pltpu.VMEM((2 * nyh * nz, owned, D // 2), F32),
                 pltpu.VMEM((D, PG), BF16),
                 dma(1), dma(4), dma(3), dma(3), dma(1), dma(1), dma(3, 2), dma(3, 2),
                 dma(3), dma(3), dma(3), dma(3), dma(1), dma(1),
                 dma(1), dma(1), dma(3), dma(3), dma(1), dma(1), dma(nx), dma(nx), dma(nyh), dma(nyh),
-                dma(nyh), dma(nyh), dma(1), dma(1), dma(1), dma(1), dma(1),
+                dma(1), dma(1), dma(1), dma(1), dma(1),
             ],
             compiler_params=pltpu.CompilerParams(
                 collective_id=0, has_side_effects=True, vmem_limit_bytes=56 * 1024 * 1024),
             cost_estimate=pl.CostEstimate(
                 flops=2 * B * D * PG * 6, bytes_accessed=2 * D * PB, transcendentals=4 * B * PG),
         )(emb, wgt)
-        return wg, eg.astype(BF16)[None]
+        return pl.pallas_call(
+            finish_outputs,
+            name="outputs",
+            out_shape=(
+                jax.ShapeDtypeStruct((1, 1, D // 4, PB), BF16),
+                jax.ShapeDtypeStruct((1, owned, D // 2), BF16),
+            ),
+            in_specs=[pl.BlockSpec(memory_space=pltpu.VMEM)] * 2,
+            out_specs=(pl.BlockSpec(memory_space=pltpu.VMEM),) * 2,
+        )(wg, eg)
 
     return jax.shard_map(
         per_device,

time: 78.2 us -> 74.7 us (0.955)
  the two profiles are of different devices: /device:TPU:1 before, /device:TPU:16 now
where the time goes in v4:
time: 74.7 us; the launch traced here: 74.6 us
  Pallas kernels  73.9 us (99%)
    pallas_call x1, Pallas kernels, per_device(): pl.pallas_call(functools.partial(kernel, chips), name='head_step', out_sh...  71.7 us
    pallas_call x1, Pallas kernels, per_device(): pl.pallas_call(finish_outputs, name='outputs', out_shape=(jax.ShapeDtypeS...  2.27 us

profile of v4, /device:TPU:16, one launch (start us, length us, event | category | flops | bytes accessed | tf_op | source)
XLA Modules:
  0.0 74.6 jit_solution(9347922233187879241)
XLA Ops:
  0.6 71.7 %head_step.1 = (bf16[1,1,128,4096]{3,2,1,0:T(8,128)(2,1)}, f32[8,256]{1,0:T(8,128)}) custom-call(bf16[1,512,512]{2,1,0:T(8,128)(2,1)} %emb.1, bf16[1,512,4096]{2,1,0:T(8,128)(2,1)} %wgt.1), custom_call_target="tpu_custom_call" | custom-call | flops 6442450944 | bytes 4194304 | tf_op jit(solution)/shard_map/head_step/pallas_call | solution.py:479
  72.3 2.3 %outputs.1 = (bf16[1,1,128,4096]{3,2,1,0:T(8,128)(2,1)}, bf16[1,8,256]{2,1,0:T(8,128)(2,1)}) custom-call(bf16[1,1,128,4096]{3,2,1,0:T(8,128)(2,1)} %get-tuple-element.4.wg, f32[8,256]{1,0:T(8,128)} %get-tuple-element.5.eg), custom_call_target="tpu_custom_call" | custom-call | tf_op jit(solution)/shard_map/outputs/pallas_call | solution.py:529

commit v5 on v4

--- a/solution.py
+++ b/solution.py
@@ -26,10 +26,10 @@
 
 def kernel(chips, emb, wgt, wg_out, eg_out,
            EB, WO, WX, KC, AB, G, ET, WT, PCS, PCR, UT, UG, RS, COLR, COLS, COL3,
-           SRC1, ALL, SRC2, AR1, AR2, AR2S, SV, R3V, EGP, RC, RX, S1, RZ, WGB,
+           SRC1, ALL, SRC2, AR1, AR2, AR2S, SV, R3V, EGP, RC, RX, S1, RZ, ZS, ZR, ZX, ZL, WGB,
            loc, w_loc, e_send, e_recv, w_send, w_recv, p_send, p_recv, a1s, a1r, a2s, a2r, b_send, b_recv,
            u_send, u_recv, v_send, v_recv, r_send, r_recv, c_send, c_recv, x_send, x_recv,
-           z_send, z_recv, g_send, g_recv, g_loc):
+           z_send, z_recv, s_send, s_recv, l_send, l_recv, g_send, g_recv, g_loc):
     nx, nyh, nz = chips
     role, p, c = (lax.axis_index(a) for a in ("role", "proto", "crop"))
     x, yh, z = p // (nyh * nz), (p // nz) % nyh, p % nz
@@ -98,6 +98,7 @@
 
         lax.fori_loop(0, PG // TILE, own_tile, 0)
 
+    S1[:, :, :, D - LANES:] = jnp.zeros(S1.shape[:3] + (LANES,), F32)
     pl.semaphore_wait(barrier, len(greeted))
 
     g_own = pl.multiple_of(c * PC + role * PG, PG)
@@ -313,6 +314,8 @@
     owned = yrows // nz
     side = half // 2
     blocks = nx // 2
+    XC = D - LANES
+    x_cols, z_cols = pl.ds(0, XC), pl.ds(XC, LANES)
 
     def side_rows(h, far):
         return pl.multiple_of(h * half + ((x // blocks) ^ far) * side, side)
@@ -354,7 +357,7 @@
                 arrived(RC.at[x_rows(m)], c_recv.at[m])
             EGP[c, rows, :] = EGP[c, rows, :] + RC[rows, :]
             if m:
-                send(EGP.at[c, rows], RX.at[h, m - 1], x_send.at[h], x_recv.at[h], at(mx=m))
+                send(EGP.at[c, rows, x_cols], RX.at[h, m - 1], x_send.at[h], x_recv.at[h], at(mx=m))
 
     expand(R3V[c], COL3, c * half)
     logit_grads(c, 1)
@@ -373,6 +376,10 @@
     send_x_parts(0, near_side)
     for h in range(1, nyh):
         send_x_parts(h, far_side + near_side)
+    for k in range(nx * nyh):
+        ZS[:, k] = EGP[c, k * yrows:(k + 1) * yrows, z_cols].reshape(nz, owned, LANES)
+    for m in z_peers:
+        send(ZS.at[z ^ m], ZR.at[m - 1], s_send.at[0], s_recv.at[0], at(mz=m))
 
     my_q = 2 * c + role
     out_first = c * PC + role * PG
@@ -392,13 +399,37 @@
         wg_out.at[0, 0, :, pl.ds(pl.multiple_of(out_first, PG), PG)], g_loc.at[0])
     mine.start()
 
+    total = ZS[z]
+    if nz > 1:
+        arrived(ZR, s_recv.at[0])
+        for m in range(nz - 1):
+            total = total + ZR[m]
+    ZX[...] = total
+
+    def give_last(mx, yh_to):
+        place = ZL.at[(mx * nyh + (yh ^ yh_to)) * 2 + (1 - role)]
+        to = {"role": 1, "proto": ((x ^ mx) * nyh + yh_to) * nz + z, "crop": c}
+        src = ZX.at[(x ^ mx) * nyh + yh_to]
+
+        def give():
+            send(src, place, l_send.at[0], l_recv.at[0], to)
+
+        if mx:
+            give()
+        else:
+            pl.when(jnp.logical_or(teacher, yh != yh_to))(give)
+
+    for m in x_peers + [0]:
+        for k in range(nyh):
+            give_last(m, k)
+
     for h in range(nyh):
         rows = pl.ds(pl.multiple_of(x * xrows + h * yrows, yrows), yrows)
         arrived(RX.at[h], x_recv.at[h])
-        total = EGP[c, rows, :]
+        total = EGP[c, rows, x_cols]
         for m in range(nx - 1):
             total = total + RX[h, m]
-        S1[h] = total.reshape(nz, owned, D)
+        S1[h, :, :, x_cols] = total.reshape(nz, owned, XC)
         my = yh ^ h
         for mz in z_peers + [0]:
             for mr in (1, 0):
@@ -419,6 +450,23 @@
     while len(parts) > 1:
         parts = [a + b for a, b in zip(parts[::2], parts[1::2])]
     eg_out[...] = parts[0]
+    others = ZL.at[pl.ds(1, 2 * nx * nyh - 1)]
+
+    @pl.when(student)
+    def _():
+        arrived(others, l_recv.at[0])
+        parts = [ZX[x * nyh + yh]] + [ZL[m] for m in range(1, 2 * nx * nyh)]
+        while len(parts) > 1:
+            parts = [a + b for a, b in zip(parts[::2], parts[1::2])]
+        eg_out[:, D // 2 - LANES:] = parts[0]
+        arrived(ZL.at[pl.ds(0, nx * nyh - 1)], l_send.at[0])
+
+    @pl.when(teacher)
+    def _():
+        arrived(ZL.at[pl.ds(0, nx * nyh)], l_send.at[0])
+
+    if nz > 1:
+        arrived(ZR, s_send.at[0])
 
     arrived(EB.at[role, my_half], e_send.at[0])
     arrived(EB.at[role, my_half], e_send.at[1])
@@ -512,14 +560,18 @@
                 pltpu.VMEM((2, vrows, LANES), F32),
                 pltpu.VMEM((2, half, D), F32),
                 pltpu.VMEM((half, D), F32),
-                pltpu.VMEM((nyh, nx - 1, yrows, D), F32),
+                pltpu.VMEM((nyh, nx - 1, yrows, D - LANES), F32),
                 pltpu.VMEM((nyh, nz, owned, D), F32),
                 pltpu.VMEM((2 * nyh * nz, owned, D // 2), F32),
+                pltpu.VMEM((nz, nx * nyh, owned, LANES), F32),
+                pltpu.VMEM((max(nz - 1, 1), nx * nyh, owned, LANES), F32),
+                pltpu.VMEM((nx * nyh, owned, LANES), F32),
+                pltpu.VMEM((2 * nx * nyh, owned, LANES), F32),
                 pltpu.VMEM((D, PG), BF16),
                 dma(1), dma(4), dma(3), dma(3), dma(1), dma(1), dma(3, 2), dma(3, 2),
                 dma(3), dma(3), dma(3), dma(3), dma(1), dma(1),
                 dma(1), dma(1), dma(3), dma(3), dma(1), dma(1), dma(nx), dma(nx), dma(nyh), dma(nyh),
-                dma(1), dma(1), dma(1), dma(1), dma(1),
+                dma(1), dma(1), dma(1), dma(1), dma(1), dma(1), dma(1), dma(1), dma(1),
             ],
             compiler_params=pltpu.CompilerParams(
                 collective_id=0, has_side_effects=True, vmem_limit_bytes=56 * 1024 * 1024),

time: 74.7 us -> 73.4 us (0.983)
  the two profiles are of different devices: /device:TPU:16 before, /device:TPU:1 now
where the time goes in v5:
time: 73.4 us; the launch traced here: 73.2 us
  Pallas kernels  72.6 us (99%)
    pallas_call x1, Pallas kernels, per_device(): pl.pallas_call(functools.partial(kernel, chips), name='head_step', out_sh...  70.3 us
    pallas_call x1, Pallas kernels, per_device(): pl.pallas_call(finish_outputs, name='outputs', out_shape=(jax.ShapeDtypeS...  2.27 us

profile of v5, /device:TPU:1, one launch (start us, length us, event | category | flops | bytes accessed | tf_op | source)
XLA Modules:
  0.0 73.2 jit_solution(6554412129703038967)
XLA Ops:
  0.6 70.3 %head_step.1 = (bf16[1,1,128,4096]{3,2,1,0:T(8,128)(2,1)}, f32[8,256]{1,0:T(8,128)}) custom-call(bf16[1,512,512]{2,1,0:T(8,128)(2,1)} %emb.1, bf16[1,512,4096]{2,1,0:T(8,128)(2,1)} %wgt.1), custom_call_target="tpu_custom_call" | custom-call | flops 6442450944 | bytes 4194304 | tf_op jit(solution)/shard_map/head_step/pallas_call | solution.py:527
  71.0 2.3 %outputs.1 = (bf16[1,1,128,4096]{3,2,1,0:T(8,128)(2,1)}, bf16[1,8,256]{2,1,0:T(8,128)(2,1)}) custom-call(bf16[1,1,128,4096]{3,2,1,0:T(8,128)(2,1)} %get-tuple-element.4.wg, f32[8,256]{1,0:T(8,128)} %get-tuple-element.5.eg), custom_call_target="tpu_custom_call" | custom-call | tf_op jit(solution)/shard_map/outputs/pallas_call | solution.py:581

commit v6 on v5

--- a/solution.py
+++ b/solution.py
@@ -585,8 +585,15 @@
                 jax.ShapeDtypeStruct((1, 1, D // 4, PB), BF16),
                 jax.ShapeDtypeStruct((1, owned, D // 2), BF16),
             ),
-            in_specs=[pl.BlockSpec(memory_space=pltpu.VMEM)] * 2,
-            out_specs=(pl.BlockSpec(memory_space=pltpu.VMEM),) * 2,
+            grid=(2,),
+            in_specs=[
+                pl.BlockSpec((1, 1, D // 8, PB), lambda k: (0, 0, k, 0)),
+                pl.BlockSpec((owned, D // 2), lambda k: (0, 0)),
+            ],
+            out_specs=(
+                pl.BlockSpec((1, 1, D // 8, PB), lambda k: (0, 0, k, 0)),
+                pl.BlockSpec((1, owned, D // 2), lambda k: (0, 0, 0)),
+            ),
         )(wg, eg)
 
     return jax.shard_map(

time: 73.4 us -> 73.2 us (level)
  no operation moved by 1% of the time
where the time goes in v6:
time: 73.2 us; the launch traced here: 73 us
  Pallas kernels  72.4 us (99%)
    pallas_call x1, Pallas kernels, per_device(): pl.pallas_call(functools.partial(kernel, chips), name='head_step', out_sh...  70.3 us
    pallas_call x1, Pallas kernels, per_device(): pl.pallas_call(finish_outputs, name='outputs', out_shape=(jax.ShapeDtypeS...  2.06 us

profile of v6, /device:TPU:1, one launch (start us, length us, event | category | flops | bytes accessed | tf_op | source)
XLA Modules:
  0.0 73.0 jit_solution(11898212077073749382)
XLA Ops:
  0.6 70.3 %head_step.1 = (bf16[1,1,128,4096]{3,2,1,0:T(8,128)(2,1)}, f32[8,256]{1,0:T(8,128)}) custom-call(bf16[1,512,512]{2,1,0:T(8,128)(2,1)} %emb.1, bf16[1,512,4096]{2,1,0:T(8,128)(2,1)} %wgt.1), custom_call_target="tpu_custom_call" | custom-call | flops 6442450944 | bytes 4194304 | tf_op jit(solution)/shard_map/head_step/pallas_call | solution.py:527
  71.0 2.1 %outputs.1 = (bf16[1,1,128,4096]{3,2,1,0:T(8,128)(2,1)}, bf16[1,8,256]{2,1,0:T(8,128)(2,1)}) custom-call(bf16[1,1,128,4096]{3,2,1,0:T(8,128)(2,1)} %get-tuple-element.4.wg, f32[8,256]{1,0:T(8,128)} %get-tuple-element.5.eg), custom_call_target="tpu_custom_call" | custom-call | tf_op jit(solution)/shard_map/outputs/pallas_call | solution.py:581

commit v7 on v6

--- a/solution.py
+++ b/solution.py
@@ -333,12 +333,7 @@
         rows = pl.ds(side_rows(h, far), side)
         local = pl.ds(pl.multiple_of(((x // blocks) ^ far) * side, side), side)
 
-        def body(j, _):
-            cols = pl.ds(pl.multiple_of(j * TILE, TILE), TILE)
-            EGP[h, local, cols] = jnp.dot(G[rows, :], WT[:, cols], preferred_element_type=F32)
-            return 0
-
-        lax.fori_loop(0, D // TILE, body, 0)
+        EGP[h, local, :] = jnp.dot(G[rows, :], WT[...], preferred_element_type=F32)
 
     def x_rows(m):
         return pl.ds(pl.multiple_of((x ^ m) * xrows, xrows), xrows)

time: 73.2 us -> 72.7 us (level)
  no operation moved by 1% of the time
where the time goes in v7:
time: 72.7 us; the launch traced here: 72.5 us
  Pallas kernels  71.9 us (99%)
    pallas_call x1, Pallas kernels, per_device(): pl.pallas_call(functools.partial(kernel, chips), name='head_step', out_sh...  69.8 us
    pallas_call x1, Pallas kernels, per_device(): pl.pallas_call(finish_outputs, name='outputs', out_shape=(jax.ShapeDtypeS...  2.06 us

profile of v7, /device:TPU:1, one launch (start us, length us, event | category | flops | bytes accessed | tf_op | source)
XLA Modules:
  0.0 72.5 jit_solution(14620450682558951700)
XLA Ops:
  0.6 69.8 %head_step.1 = (bf16[1,1,128,4096]{3,2,1,0:T(8,128)(2,1)}, f32[8,256]{1,0:T(8,128)}) custom-call(bf16[1,512,512]{2,1,0:T(8,128)(2,1)} %emb.1, bf16[1,512,4096]{2,1,0:T(8,128)(2,1)} %wgt.1), custom_call_target="tpu_custom_call" | custom-call | flops 6442450944 | bytes 4194304 | tf_op jit(solution)/shard_map/head_step/pallas_call | solution.py:522
  70.5 2.1 %outputs.1 = (bf16[1,1,128,4096]{3,2,1,0:T(8,128)(2,1)}, bf16[1,8,256]{2,1,0:T(8,128)(2,1)}) custom-call(bf16[1,1,128,4096]{3,2,1,0:T(8,128)(2,1)} %get-tuple-element.4.wg, f32[8,256]{1,0:T(8,128)} %get-tuple-element.5.eg), custom_call_target="tpu_custom_call" | custom-call | tf_op jit(solution)/shard_map/outputs/pallas_call | solution.py:576
